TPU v7x, 128 devices: a whole 4x4x4 slice. The times are simulated.
128 devices in a mesh: band: 8 (over y, core), lev: 16 (over z, x).
Axes of the slice: x: 4, y: 4, z: 4, core: 2. Of those that a mesh axis runs over, the one named last changes fastest.
Arguments:
- grid_values: bfloat16 [1024, 2, 128, 3072], P(('band', 'lev')), may hold values from -6 to 6
- lon_counts: int32 [1024], P(('band', 'lev')), may hold values from 1536 to 3072, as said below
- legendre: bfloat16 [768, 2, 1024, 384], P('lev', None, 'band'), as said below
Outputs:
- spectra: float32 [768, 2, 2, 128, 384], P('lev', None, None, 'band')
Inputs may be any that keep to these rules, and one draw needn't show every extreme that they name: `lon_counts`: A multiple of 4 for every pair, equal to 3072 for some pair. legendre[m, s, p, i] is zero where m + 2 i + s >= 768.
All inputs are finite; a program needn't handle non-finite values.
Results may differ from a plain program's by a relative error of at most 0.015.
Values may be sent and summed in bfloat16 or wider, within the bound.
A program may use at most 128 MiB of HBM per device.

v0:
```python
import math

import jax
import jax.numpy as jnp
from jax import lax
from jax.sharding import PartitionSpec as P


def fourier_table(lon_count, points, orders):
    block = math.gcd(orders, 32)
    coarse_count = orders // block
    positions = jnp.arange(points, dtype=jnp.int32)
    coarse_waves = jnp.arange(coarse_count, dtype=jnp.int32) * block
    fine_waves = jnp.arange(block, dtype=jnp.int32)
    scale_back = 1.0 / lon_count.astype(jnp.float32)
    step_angle = 2.0 * math.pi * scale_back
    coarse_angles = (coarse_waves[:, None] * positions[None, :] % lon_count).astype(
        jnp.float32
    ) * step_angle
    fine_angles = (fine_waves[:, None] * positions[None, :] % lon_count).astype(
        jnp.float32
    ) * step_angle
    coarse_cos = jnp.cos(coarse_angles)[:, None, :]
    coarse_sin = jnp.sin(coarse_angles)[:, None, :]
    fine_cos = jnp.cos(fine_angles)[None, :, :]
    fine_sin = jnp.sin(fine_angles)[None, :, :]
    joined_cos = (coarse_cos * fine_cos - coarse_sin * fine_sin).reshape(orders, points)
    joined_sin = (coarse_sin * fine_cos + coarse_cos * fine_sin).reshape(orders, points)
    inside = (positions < lon_count)[None, :]
    cosines = jnp.where(inside, joined_cos * scale_back, 0.0)
    sines = jnp.where(inside, -joined_sin * scale_back, 0.0)
    return jnp.stack([cosines, sines], axis=1).astype(jnp.bfloat16)


def on_device(grid_values, lon_counts, legendre):
    pair_count = grid_values.shape[0]
    fields = grid_values.shape[2]
    points = grid_values.shape[3]
    orders = 2 * legendre.shape[3]
    owned_orders = legendre.shape[0]
    half_orders = legendre.shape[3]
    lat_blocks = grid_values.reshape(pair_count, 2 * fields, points)

    def pair_step(pair, buffer):
        lat_rows = lax.dynamic_index_in_dim(lat_blocks, pair, 0, keepdims=False)
        lon_count = lax.dynamic_index_in_dim(lon_counts, pair, 0, keepdims=False)
        wave_table = fourier_table(lon_count, points, orders)
        spectrum = jnp.einsum(
            "mrj,kj->mrk", wave_table, lat_rows, preferred_element_type=jnp.float32
        )
        spectrum = spectrum.reshape(orders, 2, 2, fields)
        north = spectrum[:, :, 0, :]
        south = spectrum[:, :, 1, :]
        folded_pair = jnp.stack([north + south, north - south], axis=1).astype(jnp.bfloat16)
        folded_pair = folded_pair.reshape(orders, 2, 1, 2 * fields)
        return lax.dynamic_update_slice_in_dim(buffer, folded_pair, pair, 2)

    initial = jnp.zeros((orders, 2, pair_count, 2 * fields), jnp.bfloat16)
    folded_local = lax.fori_loop(0, pair_count, pair_step, initial)
    folded = lax.all_to_all(folded_local, "lev", split_axis=0, concat_axis=2, tiled=True)
    partial_sums = lax.dot_general(
        folded, legendre, (((2,), (2,)), ((0, 1), (0, 1))), preferred_element_type=jnp.float32
    ).reshape(owned_orders, 2, 2, fields, half_orders)
    return lax.psum_scatter(
        partial_sums.astype(jnp.bfloat16), "band", scatter_dimension=3, tiled=True
    ).astype(jnp.float32)


def solution(mesh):
    return jax.shard_map(
        on_device,
        mesh=mesh,
        in_specs=(
            P(("band", "lev"), None, None, None),
            P(("band", "lev")),
            P("lev", None, "band", None),
        ),
        out_specs=P("lev", None, None, "band", None),
        check_vma=False,
    )
```

profile of v0, /device:TPU:0, one launch (start us, length us, event | category | flops | bytes accessed | tf_op | source)
XLA Modules:
  0.0 474.4 jit_solution(16874772734165730768)
XLA Ops:
  6.5 252.7 %while.13 = (s32[]{:T(128)}, bf16[768,2,8,256]{0,3,2,1:T(8,128)(2,1)}, s32[8]{0:T(128)}, bf16[8,256,3072]{2,1,0:T(8,128)(2,1)}, s32[]{:T(128)}, /*index=5*/f32[]{:T(128)}, f32[]{:T(128)}, s32[]{:T(128)}) while((s32[]{:T(128)}, bf16[768,2,8,256]{0,3,2,1:T(8,128)(2,1)}, s32[8]{0:T(128)}, bf16[8,256,3072]{2,1,0:T(8,128)(2,1)}, s32[]{:T(128)}, ...), condition=%wide.region_1.2_spmd, body=%wide.region_0.1_spmd.sunk | while | flops 2469547008 | bytes 50731900 | solution.py:59
  9.8 5.2 %fusion.32 = (f32[32,3072]{1,0:T(8,128)S(1)}, f32[32,3072]{1,0:T(8,128)S(1)}) fusion(f32[]{:T(128)S(6)} %mul.482, s32[]{:T(128)S(6)} %select_n.114, pred[]{:T(512)S(6)} %lt.104), kind=kLoop, calls=%fused_computation.20.clone.1 | loop fusion | flops 983040 | bytes 786441 | tf_op jit(solution)/shard_map/while/body/eval_jaxpr/sin | solution.py:26
  15.0 4.0 fusion.33
  18.9 3.5 subtract_multiply_fusion.2
  23.1 7.2 %fusion.34 = (bf16[768,1,3072]{2,0,1:T(8,128)(2,1)}, bf16[768,1,3072]{2,0,1:T(8,128)(2,1)}) fusion(bf16[24,32,3072]{2,1,0:T(8,128)(2,1)S(1)} %get-tuple-element.142, pred[3072]{0:T(1024)(128)(4,1)S(1)} %iota_compare_fusion.2, bf16[24,32,3072]{2,1,0:T(8,128)(2,1)S(1)} %get-tuple-element.143), kind=kLoop, calls=%fused_computation.7.clone.1 | loop fusion | flops 4718592 | bytes 18877440 | tf_op jit(solution)/shard_map/convert.4
  31.7 5.3 %fusion.35 = f32[768,2,2,128]{0,3,2,1:T(8,128)S(1)} fusion(bf16[2,128,3072,1]{2,1,0,3:T(8,128)(2,1)S(1)} %bitcast.46, bf16[768,1,3072]{2,0,1:T(8,128)(2,1)} %get-tuple-element.144, bf16[768,1,3072]{2,0,1:T(8,128)(2,1)} %get-tuple-element.145), kind=kOutput, calls=%fused_computation.1.clone.1 | convolution fusion | flops 2434793472 | bytes 12582912 | tf_op jit(solution)/shard_map/while/body/eval_jaxpr/mrj,kj->mrk/dot_general | solution.py:48
  41.3 5.2 %fusion.32 = (f32[32,3072]{1,0:T(8,128)S(1)}, f32[32,3072]{1,0:T(8,128)S(1)}) fusion(f32[]{:T(128)S(6)} %mul.482, s32[]{:T(128)S(6)} %select_n.114, pred[]{:T(512)S(6)} %lt.104), kind=kLoop, calls=%fused_computation.20.clone.1 | loop fusion | flops 983040 | bytes 786441 | tf_op jit(solution)/shard_map/while/body/eval_jaxpr/sin | solution.py:26
  46.5 4.0 fusion.33
  50.5 3.5 subtract_multiply_fusion.2
  54.6 7.2 %fusion.34 = (bf16[768,1,3072]{2,0,1:T(8,128)(2,1)}, bf16[768,1,3072]{2,0,1:T(8,128)(2,1)}) fusion(bf16[24,32,3072]{2,1,0:T(8,128)(2,1)S(1)} %get-tuple-element.142, pred[3072]{0:T(1024)(128)(4,1)S(1)} %iota_compare_fusion.2, bf16[24,32,3072]{2,1,0:T(8,128)(2,1)S(1)} %get-tuple-element.143), kind=kLoop, calls=%fused_computation.7.clone.1 | loop fusion | flops 4718592 | bytes 18877440 | tf_op jit(solution)/shard_map/convert.4
  61.8 1.5 constant_dynamic-slice_fusion.2
  63.3 5.3 %fusion.35 = f32[768,2,2,128]{0,3,2,1:T(8,128)S(1)} fusion(bf16[2,128,3072,1]{2,1,0,3:T(8,128)(2,1)S(1)} %bitcast.46, bf16[768,1,3072]{2,0,1:T(8,128)(2,1)} %get-tuple-element.144, bf16[768,1,3072]{2,0,1:T(8,128)(2,1)} %get-tuple-element.145), kind=kOutput, calls=%fused_computation.1.clone.1 | convolution fusion | flops 2434793472 | bytes 12582912 | tf_op jit(solution)/shard_map/while/body/eval_jaxpr/mrj,kj->mrk/dot_general | solution.py:48
  72.9 5.2 %fusion.32 = (f32[32,3072]{1,0:T(8,128)S(1)}, f32[32,3072]{1,0:T(8,128)S(1)}) fusion(f32[]{:T(128)S(6)} %mul.482, s32[]{:T(128)S(6)} %select_n.114, pred[]{:T(512)S(6)} %lt.104), kind=kLoop, calls=%fused_computation.20.clone.1 | loop fusion | flops 983040 | bytes 786441 | tf_op jit(solution)/shard_map/while/body/eval_jaxpr/sin | solution.py:26
  78.1 4.0 fusion.33
  82.1 3.5 subtract_multiply_fusion.2
  86.2 7.2 %fusion.34 = (bf16[768,1,3072]{2,0,1:T(8,128)(2,1)}, bf16[768,1,3072]{2,0,1:T(8,128)(2,1)}) fusion(bf16[24,32,3072]{2,1,0:T(8,128)(2,1)S(1)} %get-tuple-element.142, pred[3072]{0:T(1024)(128)(4,1)S(1)} %iota_compare_fusion.2, bf16[24,32,3072]{2,1,0:T(8,128)(2,1)S(1)} %get-tuple-element.143), kind=kLoop, calls=%fused_computation.7.clone.1 | loop fusion | flops 4718592 | bytes 18877440 | tf_op jit(solution)/shard_map/convert.4
  94.9 5.3 %fusion.35 = f32[768,2,2,128]{0,3,2,1:T(8,128)S(1)} fusion(bf16[2,128,3072,1]{2,1,0,3:T(8,128)(2,1)S(1)} %bitcast.46, bf16[768,1,3072]{2,0,1:T(8,128)(2,1)} %get-tuple-element.144, bf16[768,1,3072]{2,0,1:T(8,128)(2,1)} %get-tuple-element.145), kind=kOutput, calls=%fused_computation.1.clone.1 | convolution fusion | flops 2434793472 | bytes 12582912 | tf_op jit(solution)/shard_map/while/body/eval_jaxpr/mrj,kj->mrk/dot_general | solution.py:48
  104.5 5.2 %fusion.32 = (f32[32,3072]{1,0:T(8,128)S(1)}, f32[32,3072]{1,0:T(8,128)S(1)}) fusion(f32[]{:T(128)S(6)} %mul.482, s32[]{:T(128)S(6)} %select_n.114, pred[]{:T(512)S(6)} %lt.104), kind=kLoop, calls=%fused_computation.20.clone.1 | loop fusion | flops 983040 | bytes 786441 | tf_op jit(solution)/shard_map/while/body/eval_jaxpr/sin | solution.py:26
  109.7 4.0 fusion.33
  113.7 3.5 subtract_multiply_fusion.2
  117.8 7.2 %fusion.34 = (bf16[768,1,3072]{2,0,1:T(8,128)(2,1)}, bf16[768,1,3072]{2,0,1:T(8,128)(2,1)}) fusion(bf16[24,32,3072]{2,1,0:T(8,128)(2,1)S(1)} %get-tuple-element.142, pred[3072]{0:T(1024)(128)(4,1)S(1)} %iota_compare_fusion.2, bf16[24,32,3072]{2,1,0:T(8,128)(2,1)S(1)} %get-tuple-element.143), kind=kLoop, calls=%fused_computation.7.clone.1 | loop fusion | flops 4718592 | bytes 18877440 | tf_op jit(solution)/shard_map/convert.4
  126.4 5.3 %fusion.35 = f32[768,2,2,128]{0,3,2,1:T(8,128)S(1)} fusion(bf16[2,128,3072,1]{2,1,0,3:T(8,128)(2,1)S(1)} %bitcast.46, bf16[768,1,3072]{2,0,1:T(8,128)(2,1)} %get-tuple-element.144, bf16[768,1,3072]{2,0,1:T(8,128)(2,1)} %get-tuple-element.145), kind=kOutput, calls=%fused_computation.1.clone.1 | convolution fusion | flops 2434793472 | bytes 12582912 | tf_op jit(solution)/shard_map/while/body/eval_jaxpr/mrj,kj->mrk/dot_general | solution.py:48
  136.1 5.2 %fusion.32 = (f32[32,3072]{1,0:T(8,128)S(1)}, f32[32,3072]{1,0:T(8,128)S(1)}) fusion(f32[]{:T(128)S(6)} %mul.482, s32[]{:T(128)S(6)} %select_n.114, pred[]{:T(512)S(6)} %lt.104), kind=kLoop, calls=%fused_computation.20.clone.1 | loop fusion | flops 983040 | bytes 786441 | tf_op jit(solution)/shard_map/while/body/eval_jaxpr/sin | solution.py:26
  141.3 4.0 fusion.33
  145.3 3.5 subtract_multiply_fusion.2
  149.4 7.2 %fusion.34 = (bf16[768,1,3072]{2,0,1:T(8,128)(2,1)}, bf16[768,1,3072]{2,0,1:T(8,128)(2,1)}) fusion(bf16[24,32,3072]{2,1,0:T(8,128)(2,1)S(1)} %get-tuple-element.142, pred[3072]{0:T(1024)(128)(4,1)S(1)} %iota_compare_fusion.2, bf16[24,32,3072]{2,1,0:T(8,128)(2,1)S(1)} %get-tuple-element.143), kind=kLoop, calls=%fused_computation.7.clone.1 | loop fusion | flops 4718592 | bytes 18877440 | tf_op jit(solution)/shard_map/convert.4
  156.5 1.5 constant_dynamic-slice_fusion.2
  158.0 5.3 %fusion.35 = f32[768,2,2,128]{0,3,2,1:T(8,128)S(1)} fusion(bf16[2,128,3072,1]{2,1,0,3:T(8,128)(2,1)S(1)} %bitcast.46, bf16[768,1,3072]{2,0,1:T(8,128)(2,1)} %get-tuple-element.144, bf16[768,1,3072]{2,0,1:T(8,128)(2,1)} %get-tuple-element.145), kind=kOutput, calls=%fused_computation.1.clone.1 | convolution fusion | flops 2434793472 | bytes 12582912 | tf_op jit(solution)/shard_map/while/body/eval_jaxpr/mrj,kj->mrk/dot_general | solution.py:48
  167.7 5.2 %fusion.32 = (f32[32,3072]{1,0:T(8,128)S(1)}, f32[32,3072]{1,0:T(8,128)S(1)}) fusion(f32[]{:T(128)S(6)} %mul.482, s32[]{:T(128)S(6)} %select_n.114, pred[]{:T(512)S(6)} %lt.104), kind=kLoop, calls=%fused_computation.20.clone.1 | loop fusion | flops 983040 | bytes 786441 | tf_op jit(solution)/shard_map/while/body/eval_jaxpr/sin | solution.py:26
  172.9 4.0 fusion.33
  176.9 3.5 subtract_multiply_fusion.2
  181.0 7.2 %fusion.34 = (bf16[768,1,3072]{2,0,1:T(8,128)(2,1)}, bf16[768,1,3072]{2,0,1:T(8,128)(2,1)}) fusion(bf16[24,32,3072]{2,1,0:T(8,128)(2,1)S(1)} %get-tuple-element.142, pred[3072]{0:T(1024)(128)(4,1)S(1)} %iota_compare_fusion.2, bf16[24,32,3072]{2,1,0:T(8,128)(2,1)S(1)} %get-tuple-element.143), kind=kLoop, calls=%fused_computation.7.clone.1 | loop fusion | flops 4718592 | bytes 18877440 | tf_op jit(solution)/shard_map/convert.4
  189.6 5.3 %fusion.35 = f32[768,2,2,128]{0,3,2,1:T(8,128)S(1)} fusion(bf16[2,128,3072,1]{2,1,0,3:T(8,128)(2,1)S(1)} %bitcast.46, bf16[768,1,3072]{2,0,1:T(8,128)(2,1)} %get-tuple-element.144, bf16[768,1,3072]{2,0,1:T(8,128)(2,1)} %get-tuple-element.145), kind=kOutput, calls=%fused_computation.1.clone.1 | convolution fusion | flops 2434793472 | bytes 12582912 | tf_op jit(solution)/shard_map/while/body/eval_jaxpr/mrj,kj->mrk/dot_general | solution.py:48
  199.3 5.2 %fusion.32 = (f32[32,3072]{1,0:T(8,128)S(1)}, f32[32,3072]{1,0:T(8,128)S(1)}) fusion(f32[]{:T(128)S(6)} %mul.482, s32[]{:T(128)S(6)} %select_n.114, pred[]{:T(512)S(6)} %lt.104), kind=kLoop, calls=%fused_computation.20.clone.1 | loop fusion | flops 983040 | bytes 786441 | tf_op jit(solution)/shard_map/while/body/eval_jaxpr/sin | solution.py:26
  204.5 4.0 fusion.33
  208.4 3.5 subtract_multiply_fusion.2
  212.6 7.2 %fusion.34 = (bf16[768,1,3072]{2,0,1:T(8,128)(2,1)}, bf16[768,1,3072]{2,0,1:T(8,128)(2,1)}) fusion(bf16[24,32,3072]{2,1,0:T(8,128)(2,1)S(1)} %get-tuple-element.142, pred[3072]{0:T(1024)(128)(4,1)S(1)} %iota_compare_fusion.2, bf16[24,32,3072]{2,1,0:T(8,128)(2,1)S(1)} %get-tuple-element.143), kind=kLoop, calls=%fused_computation.7.clone.1 | loop fusion | flops 4718592 | bytes 18877440 | tf_op jit(solution)/shard_map/convert.4
  221.2 5.3 %fusion.35 = f32[768,2,2,128]{0,3,2,1:T(8,128)S(1)} fusion(bf16[2,128,3072,1]{2,1,0,3:T(8,128)(2,1)S(1)} %bitcast.46, bf16[768,1,3072]{2,0,1:T(8,128)(2,1)} %get-tuple-element.144, bf16[768,1,3072]{2,0,1:T(8,128)(2,1)} %get-tuple-element.145), kind=kOutput, calls=%fused_computation.1.clone.1 | convolution fusion | flops 2434793472 | bytes 12582912 | tf_op jit(solution)/shard_map/while/body/eval_jaxpr/mrj,kj->mrk/dot_general | solution.py:48
  230.9 5.2 %fusion.32 = (f32[32,3072]{1,0:T(8,128)S(1)}, f32[32,3072]{1,0:T(8,128)S(1)}) fusion(f32[]{:T(128)S(6)} %mul.482, s32[]{:T(128)S(6)} %select_n.114, pred[]{:T(512)S(6)} %lt.104), kind=kLoop, calls=%fused_computation.20.clone.1 | loop fusion | flops 983040 | bytes 786441 | tf_op jit(solution)/shard_map/while/body/eval_jaxpr/sin | solution.py:26
  236.0 4.0 fusion.33
  240.0 3.5 subtract_multiply_fusion.2
  244.1 7.2 %fusion.34 = (bf16[768,1,3072]{2,0,1:T(8,128)(2,1)}, bf16[768,1,3072]{2,0,1:T(8,128)(2,1)}) fusion(bf16[24,32,3072]{2,1,0:T(8,128)(2,1)S(1)} %get-tuple-element.142, pred[3072]{0:T(1024)(128)(4,1)S(1)} %iota_compare_fusion.2, bf16[24,32,3072]{2,1,0:T(8,128)(2,1)S(1)} %get-tuple-element.143), kind=kLoop, calls=%fused_computation.7.clone.1 | loop fusion | flops 4718592 | bytes 18877440 | tf_op jit(solution)/shard_map/convert.4
  252.8 5.3 %fusion.35 = f32[768,2,2,128]{0,3,2,1:T(8,128)S(1)} fusion(bf16[2,128,3072,1]{2,1,0,3:T(8,128)(2,1)S(1)} %bitcast.46, bf16[768,1,3072]{2,0,1:T(8,128)(2,1)} %get-tuple-element.144, bf16[768,1,3072]{2,0,1:T(8,128)(2,1)} %get-tuple-element.145), kind=kOutput, calls=%fused_computation.1.clone.1 | convolution fusion | flops 2434793472 | bytes 12582912 | tf_op jit(solution)/shard_map/while/body/eval_jaxpr/mrj,kj->mrk/dot_general | solution.py:48
  259.2 9.1 %copy.5 = bf16[768,2,8,256]{3,2,1,0:T(8,128)(2,1)} copy(bf16[768,2,8,256]{0,3,2,1:T(8,128)(2,1)} %get-tuple-element.84) | data formatting | bytes 12582912 | tf_op jit(solution)/shard_map/while | solution.py:59
  268.3 81.4 %all_to_all.18 = bf16[768,2,8,256]{3,2,1,0:T(8,128)(2,1)} all-to-all(bf16[768,2,8,256]{3,2,1,0:T(8,128)(2,1)} %copy.5), channel_id=1, replica_groups=mesh['band'=8,'lev'=16] {'lev'}, dimensions={0} | all-to-all | bytes 12582912 | tf_op jit(solution)/shard_map/all_to_all | solution.py:60
  349.7 13.9 %convolution_convert_fusion = bf16[48,2,256,384]{3,2,1,0:T(8,128)(2,1)} fusion(bf16[48,2,128,384]{3,2,1,0:T(8,128)(2,1)} %param.7, bf16[48,2,16,8,256]{4,3,1,0,2:T(8,128)(2,1)} %bitcast.47), kind=kOutput, calls=%fused_computation.37 | convolution fusion | flops 2425356288 | bytes 34603008 | tf_op jit(solution)/shard_map/dot_general | solution.py:61
  363.6 99.5 %reduce-scatter.2.cloned.1.call-done = bf16[48,2,2,16,384]{4,3,2,1,0:T(8,128)(2,1)} async-done(((bf16[48,2,2,128,384]{4,3,2,1,0:T(8,128)(2,1)}), bf16[48,2,2,16,384]{4,3,2,1,0:T(8,128)(2,1)}) %reduce-scatter.2.cloned.1.call-update) | async-done | bytes 2359312 | tf_op jit(solution)/shard_map/reduce_scatter | solution.py:64
  463.1 4.5 convert_element_type.67
  (49 shorter events, 33.2 us)
Async XLA Ops:
  6.5 456.6 %reduce-scatter.2.cloned.1.call-start = ((), (), s32[]{:S(2)}) async-start(), calls=%async_computation.2 | async-start | bytes 21233664 | tf_op jit(solution)/shard_map/reduce_scatter | solution.py:64
Sparse Core Ops, SparseCore 0:
  363.8 99.2 reduce-scatter.1
where the time goes:
time: 476 us; the launch traced here: 474 us
  other arithmetic  177 us (37%)
  waiting for transfers between devices  99.5 us (21%)
  blocking collectives  81.4 us (17%)
  matrix products  56.1 us (12%)
  local copies, waits for them, and re-layouts  31.1 us (7%)
  loops' own time  16.2 us (3%)
  between operations  13.4 us (3%)
    reduce_scatter x1, waiting for transfers between devices, on_device(): lax.psum_scatter(partial_sums.astype(jnp.bfloat16), 'band', scatter_dimen...  99.5 us
    all_to_all x1, blocking collectives, on_device(): lax.all_to_all(folded_local, 'lev', split_axis=0, concat_axis=2, tiled=True)  81.4 us
    another operation x16, other arithmetic  58.5 us
    dot_general x8, matrix products, pair_step(): jnp.einsum('mrj,kj->mrk', wave_table, lat_rows, preferred_element_type=jn...  42.2 us
    sin x8, other arithmetic, fourier_table(): fine_sin = jnp.sin(fine_angles)[None, :, :]  41.5 us
    cos x8, other arithmetic, fourier_table(): coarse_cos = jnp.cos(coarse_angles)[:, None, :]  31.8 us
    mul x8, other arithmetic, fourier_table(): cosines = jnp.where(inside, joined_cos * scale_back, 0.0)  27.7 us
    another operation x1, loops' own time, on_device(): folded_local = lax.fori_loop(0, pair_count, pair_step, initial)  16.2 us
  transfers between devices with their start and end apart: 1, of which 1 were waited for; matrix products, arithmetic and copies ran while one was open for 0% of the time, Pallas kernels for 0%

commit v1 on v0

v1 whole, which is shorter than its diff:
```python
import functools

import jax
import jax.numpy as jnp
from jax import lax
from jax.experimental import pallas as pl
from jax.experimental.pallas import tpu as pltpu
from jax.sharding import PartitionSpec as P

F32 = jnp.float32
BF16 = jnp.bfloat16
COS = (1.0, -19.73920440673828, 64.9390869140625, -85.4496078491211, 60.16310119628906, -25.950063705444336, 6.50340461730957)
SIN = (6.283182621002197, -41.341392517089844, 81.59541320800781, -76.57229614257812, 41.17121124267578, -12.217327117919922)
LANES = 128


def poly(coefs, z):
    out = jnp.full_like(z, coefs[-1])
    for coef in coefs[-2::-1]:
        out = out * z + coef
    return out


def cos_sin(products, count, inverse):
    turns = jnp.floor(products * inverse + 0.5)
    t = (products - turns * count) * inverse
    z = t * t
    return poly(COS, z), t * poly(SIN, z)


def prepare_kernel(owners, owned, counts_ref, inverse_ref, x_ref, y_ref, coarse_ref, fine_ref):
    pair = pl.program_id(0)
    count = counts_ref[pair]
    quarter = lax.shift_right_logical(count, 2)
    fields, points = x_ref.shape[1:]
    width = points // 4
    tiles = width // LANES
    last = points - width - LANES
    rows = 16
    lane = lax.broadcasted_iota(jnp.int32, (rows, LANES), 1)
    starts, shifts = [], []
    for k in range(4):
        start = jnp.minimum(quarter * k // LANES * LANES, last)
        starts.append(start)
        shifts.append(quarter * k - start)

    def fold(step, carry):
        row = pl.ds(pl.multiple_of(step * rows, rows), rows)
        pieces = []
        for k in range(4):
            shift = shifts[k]
            both = []
            for h in range(2):
                turned = []
                for i in range(tiles + (k > 0)):
                    at = pl.multiple_of(starts[k] + i * LANES, LANES)
                    v = x_ref[h, row, pl.ds(at, LANES)].astype(F32)
                    if k:
                        v = pltpu.roll(v, (LANES - shift) & (LANES - 1), 1)
                    turned.append(v)
                if k:
                    keep = lane < LANES - shift
                    turned = [jnp.where(keep, turned[i], turned[i + 1]) for i in range(tiles)]
                both.append(turned)
            pieces.append([[n + s for n, s in zip(*both)], [n - s for n, s in zip(*both)]])
        for s in range(2):
            to = pl.ds(pl.multiple_of(step * rows + s * fields, rows), rows)
            for i in range(tiles):
                inside = lane + i * LANES < quarter
                x0, x1, x2, x3 = (jnp.where(inside, pieces[k][s][i], 0.0) for k in range(4))
                at = pl.ds(i * LANES, LANES)
                y_ref[0, to, at] = ((x0 + x2) + (x1 + x3)).astype(BF16)
                y_ref[1, to, at] = (x0 - x2).astype(BF16)
                y_ref[2, to, at] = ((x0 + x2) - (x1 + x3)).astype(BF16)
                y_ref[3, to, at] = (x1 - x3).astype(BF16)
        return carry

    lax.fori_loop(0, fields // rows, fold, 0)

    n = count.astype(F32)
    inverse = inverse_ref[pair]
    groups = owned // 4
    middle = 2 * groups - 2
    place = lax.broadcasted_iota(jnp.int32, (16, width), 1).astype(F32)
    row = lax.broadcasted_iota(jnp.int32, (16, width), 0).astype(F32)
    for step in range(groups // 2):
        c, s = cos_sin(place * float(4 * step + 2), n, inverse)
        fine_ref[step, 0] = c.astype(BF16)
        fine_ref[step, 1] = s.astype(BF16)
    owner_cos, owner_sin = cos_sin(place * (row * float(owned)), n, inverse)
    owner_cos, owner_sin = owner_cos * inverse, owner_sin * inverse
    for u in range(4):
        c, s = cos_sin(place * float(middle + u), n, inverse)
        coarse_ref[u, 0] = (owner_cos * c - owner_sin * s).astype(BF16)
        coarse_ref[u, 1] = (owner_sin * c + owner_cos * s).astype(BF16)


def prepare(grid_values, lon_counts, owners, owned):
    pairs, _, fields, points = grid_values.shape
    width = points // 4
    halves = owned // 8
    smem = pl.BlockSpec(memory_space=pltpu.SMEM)
    return pl.pallas_call(
        functools.partial(prepare_kernel, owners, owned),
        grid=(pairs,),
        out_shape=(
            jax.ShapeDtypeStruct((pairs, 4, 2 * fields, width), BF16),
            jax.ShapeDtypeStruct((pairs, 4, 2, owners, width), BF16),
            jax.ShapeDtypeStruct((pairs, halves, 2, owners, width), BF16),
        ),
        in_specs=[smem, smem, pl.BlockSpec((None, 2, fields, points), lambda p: (p, 0, 0, 0))],
        out_specs=(
            pl.BlockSpec((None, 4, 2 * fields, width), lambda p: (p, 0, 0, 0)),
            pl.BlockSpec((None, 4, 2, owners, width), lambda p: (p, 0, 0, 0, 0)),
            pl.BlockSpec((None, halves, 2, owners, width), lambda p: (p, 0, 0, 0, 0)),
        ),
        compiler_params=pltpu.CompilerParams(vmem_limit_bytes=48 * 2**20),
    )(lon_counts, 1.0 / lon_counts.astype(F32), grid_values)


def transform_kernel(u, *refs):
    if u % 2:
        a_ref, b_ref, coarse_ref, fine_ref, out_ref, table, total = refs
        sources = (a_ref, b_ref)
    else:
        a_ref, coarse_ref, fine_ref, out_ref, table, total = refs
        sources = (a_ref,)
    pair = pl.program_id(0)
    pairs = pl.num_programs(0)
    halves = fine_ref.shape[0]
    owners = coarse_ref.shape[1]
    for step in range(halves):
        for j, (k, l) in enumerate(((0, 0), (1, 0), (0, 1), (1, 1))):
            table[pl.ds((4 * step + j) * owners, owners), :] = coarse_ref[k] * fine_ref[step, l]
    sums = [
        lax.dot_general(table[...], ref[...], (((1,), (1,)), ((), ())), preferred_element_type=F32)
        for ref in sources
    ]
    spot = pl.ds(pair, owners, stride=8)
    fields = out_ref.shape[-1]

    def keep(t, real, imag):
        for r, value in enumerate((real, imag)):
            for s in range(2):
                total[4 * t + 2 * r + s, spot, :] = value[:, s * fields : (s + 1) * fields]

    for step in range(halves):
        waves = []
        for part in sums:
            cc, sc, cs, ss = (part[(4 * step + j) * owners : (4 * step + j + 1) * owners] for j in range(4))
            waves.append((cc - ss, sc + cs, cc + ss, sc - cs))
        if u % 2:
            (ca, sa, da, ta), (cb, sb, db, tb) = waves
            if u == 1:
                keep(halves + step, ca - sb, -(sa + cb))
                keep(halves - 1 - step, da - tb, -(ta + db))
            else:
                keep(halves + step, ca + sb, cb - sa)
                keep(halves - 1 - step, da + tb, db - ta)
        else:
            ((ca, sa, da, ta),) = waves
            keep(halves + step, ca, -sa)
            keep(halves - 1 - step, da, -ta)

    @pl.when(pair == pairs - 1)
    def _():
        for t in range(2 * halves):
            for s in range(2):
                real = total[4 * t + s].reshape(owners, 8, fields)
                imag = total[4 * t + 2 + s].reshape(owners, 8, fields)
                out_ref[:, t, s] = jnp.concatenate([real, imag], axis=1).astype(BF16)


def transform(u, y, coarse, fine):
    pairs, _, columns, width = y.shape
    halves, _, owners = fine.shape[1:4]
    fields = columns // 2
    used = (1, 3) if u % 2 else (u,)
    return pl.pallas_call(
        functools.partial(transform_kernel, u),
        grid=(pairs,),
        out_shape=jax.ShapeDtypeStruct((owners, 2 * halves, 2, 2 * pairs, fields), BF16),
        in_specs=[pl.BlockSpec((None, None, columns, width), functools.partial(lambda k, p: (p, k, 0, 0), k)) for k in used]
        + [
            pl.BlockSpec((None, None, 2, owners, width), lambda p: (p, u, 0, 0, 0)),
            pl.BlockSpec((None, halves, 2, owners, width), lambda p: (p, 0, 0, 0, 0)),
        ],
        out_specs=pl.BlockSpec((owners, 2 * halves, 2, 2 * pairs, fields), lambda p: (0, 0, 0, 0, 0)),
        scratch_shapes=[
            pltpu.VMEM((4 * halves * owners, width), BF16),
            pltpu.VMEM((8 * halves, owners * pairs, fields), F32),
        ],
        compiler_params=pltpu.CompilerParams(vmem_limit_bytes=48 * 2**20),
    )(*[y] * len(used), coarse, fine)


def legendre_kernel(f_ref, l_ref, out_ref):
    owners, _, both, fields = f_ref.shape
    pairs = both // 2
    for s in range(2):
        f = f_ref[:, s].astype(F32).reshape(owners, 2, pairs, fields)
        for r in range(2):
            part = f[:, r].reshape(owners * pairs, fields).astype(BF16)
            out_ref[s, r] = lax.dot_general(
                part, l_ref[s], (((0,), (0,)), ((), ())), preferred_element_type=F32
            ).astype(BF16)


def legendre_sums(u, folded, legendre):
    owners, groups, _, both, fields = folded.shape
    _, _, _, latitudes, degrees = legendre.shape
    return pl.pallas_call(
        legendre_kernel,
        grid=(groups,),
        out_shape=jax.ShapeDtypeStruct((groups, 2, 2, fields, degrees), BF16),
        in_specs=[
            pl.BlockSpec((owners, None, 2, both, fields), lambda k: (0, k, 0, 0, 0)),
            pl.BlockSpec((None, None, 2, latitudes, degrees), lambda k: (k, u, 0, 0, 0)),
        ],
        out_specs=pl.BlockSpec((None, 2, 2, fields, degrees), lambda k: (k, 0, 0, 0, 0)),
        compiler_params=pltpu.CompilerParams(vmem_limit_bytes=48 * 2**20),
    )(folded, legendre)


def on_device(owners, grid_values, lon_counts, legendre):
    owned = legendre.shape[0]
    y, coarse, fine = prepare(grid_values, lon_counts, owners, owned)
    by_class = legendre.reshape(owned // 4, 4, *legendre.shape[1:])
    results = []
    for u in range(4):
        chunk = transform(u, y, coarse, fine)
        folded = lax.all_to_all(chunk, "lev", split_axis=0, concat_axis=0, tiled=True)
        partial_sums = legendre_sums(u, folded, by_class)
        results.append(lax.psum_scatter(partial_sums, "band", scatter_dimension=3, tiled=True))
    spectra = jnp.stack(results, axis=1)
    return spectra.reshape(owned, *spectra.shape[2:]).astype(F32)


def solution(mesh):
    return jax.shard_map(
        functools.partial(on_device, mesh.shape["lev"]),
        mesh=mesh,
        in_specs=(
            P(("band", "lev"), None, None, None),
            P(("band", "lev")),
            P("lev", None, "band", None),
        ),
        out_specs=P("lev", None, None, "band", None),
        check_vma=False,
    )
```

time: 476 us -> 248 us (0.52)
  other arithmetic: 177 us -> 2.66 us
  Pallas kernels: 0 us -> 83.8 us
  waiting for transfers between devices: 99.5 us -> 36.8 us
  matrix products: 56.1 us -> 0 us
  local copies, waits for them, and re-layouts: 31.1 us -> 7.7 us
  blocking collectives: 81.4 us -> 102 us
  loops' own time: 16.2 us -> 0 us
    pallas_call x0 -> x9, Pallas kernels: none -> 83.8 us  [the longest x4 38.5 us: legendre_sums(): pl.pallas_call(legendre_kernel, grid=(groups,), out_shape=jax.ShapeDtypeS...]
    reduce_scatter x1 -> x4, waiting for transfers between devices: 99.5 us -> 36.7 us  [on_device(): lax.psum_scatter(partial_sums, 'band', scatter_dimension=3, tiled=True)]
    another operation x16 -> x0, other arithmetic: 58.5 us -> none
    dot_general x9 -> x0, matrix products: 56.1 us -> none  [the longest x8 42.2 us: pair_step(): jnp.einsum('mrj,kj->mrk', wave_table, lat_rows, preferred_element_type=jn...]
    sin x8 -> x0, other arithmetic: 41.5 us -> none  [fourier_table(): fine_sin = jnp.sin(fine_angles)[None, :, :]]
    cos x8 -> x0, other arithmetic: 31.8 us -> none  [fourier_table(): coarse_cos = jnp.cos(coarse_angles)[:, None, :]]
    mul x16 -> x0, other arithmetic: 27.7 us -> none  [the longest x8 27.7 us: fourier_table(): cosines = jnp.where(inside, joined_cos * scale_back, 0.0)]
    dynamic_slice x16 -> x0, local copies, waits for them, and re-layouts: 22 us -> none  [the longest x8 12.1 us: pair_step(): lat_rows = lax.dynamic_index_in_dim(lat_blocks, pair, 0, keepdims=False)]
  transfers between devices with their start and end apart: 1 -> 4, of which waited for: 1 -> 1; matrix products, arithmetic and copies ran while one was open for 0% -> 0% of each run, Pallas kernels for 0% -> 20%
where the time goes in v1:
time: 248 us; the launch traced here: 246 us
  blocking collectives  102 us (41%)
  Pallas kernels  83.8 us (34%)
  waiting for transfers between devices  36.8 us (15%)
  between operations  13.2 us (5%)
  local copies, waits for them, and re-layouts  7.7 us (3%)
  other arithmetic  2.66 us (1%)
    all_to_all x4, blocking collectives, on_device(): lax.all_to_all(chunk, 'lev', split_axis=0, concat_axis=0, tiled=True)  102 us
    pallas_call x4, Pallas kernels, legendre_sums(): pl.pallas_call(legendre_kernel, grid=(groups,), out_shape=jax.ShapeDtypeS...  38.5 us
    reduce_scatter x4, waiting for transfers between devices, on_device(): lax.psum_scatter(partial_sums, 'band', scatter_dimension=3, tiled=True)  36.7 us
    pallas_call x4, Pallas kernels, transform(): pl.pallas_call(functools.partial(transform_kernel, u), grid=(pairs,), out...  29 us
    pallas_call x1, Pallas kernels, prepare(): pl.pallas_call(functools.partial(prepare_kernel, owners, owned), grid=(pa...  16.3 us
  transfers between devices with their start and end apart: 4, of which 1 were waited for; matrix products, arithmetic and copies ran while one was open for 0% of the time, Pallas kernels for 20%

profile of v1, /device:TPU:0, one launch (start us, length us, event | category | flops | bytes accessed | tf_op | source)
XLA Modules:
  0.0 246.0 jit_solution(16691800051155895884)
XLA Ops:
  6.5 0.0 reduce-scatter.7.cloned.1.call-start
  6.5 0.7 convert_divide_fusion.inverse_ref
  7.2 0.0 copy-start.4
  7.2 0.7 copy-done.4
  7.9 16.3 %shard_map.37 = (bf16[8,4,256,768]{3,2,1,0:T(8,128)(2,1)}, bf16[8,4,2,16,768]{4,3,2,1,0:T(8,128)(2,1)S(1)}, bf16[8,6,2,16,768]{4,3,2,1,0:T(8,128)(2,1)S(1)}) custom-call(s32[8]{0:T(128)S(1)} %copy-done.4, f32[8]{0:T(128)S(1)} %convert_divide_fusion.inverse_ref, bf16[8,2,128,3072]{3,2,1,0:T(8,128)(2,1)} %x_ref.1), custom_call_target="tpu_custom_call" | custom-call | tf_op jit(solution)/shard_map/pallas_call | solution.py:103
  24.2 0.0 copy-start
  24.2 8.2 %shard_map.40 = bf16[16,12,2,16,128]{4,3,2,1,0:T(8,128)(2,1)S(1)} custom-call(bf16[8,4,256,768]{3,2,1,0:T(8,128)(2,1)} %get-tuple-element.8.refs_0_.refs_1_, bf16[8,4,256,768]{3,2,1,0:T(8,128)(2,1)} %get-tuple-element.8.refs_0_.refs_1_, bf16[8,4,2,16,768]{4,3,2,1,0:T(8,128)(2,1)S(1)} %get-tuple-element.9.refs_1_.refs_2_, ...), custom_call_target="tpu_custom_call" | custom-call | tf_op jit(solution)/shard_map/pallas_call | solution.py:179
  32.4 0.0 copy-done
  32.4 30.5 %all_to_all.20.f_ref = bf16[16,12,2,16,128]{4,3,2,1,0:T(8,128)(2,1)S(1)} all-to-all(bf16[16,12,2,16,128]{4,3,2,1,0:T(8,128)(2,1)S(1)} %shard_map.40), channel_id=1, replica_groups=mesh['band'=8,'lev'=16] {'lev'}, dimensions={0} | all-to-all | bytes 3145728 | tf_op jit(solution)/shard_map/all_to_all | solution.py:232
  62.9 9.6 %shard_map.41 = bf16[12,2,2,128,384]{4,3,2,1,0:T(8,128)(2,1)} custom-call(bf16[16,12,2,16,128]{4,3,2,1,0:T(8,128)(2,1)S(1)} %all_to_all.20.f_ref, bf16[12,4,2,128,384]{4,3,2,1,0:T(8,128)(2,1)} %bitcast.6), custom_call_target="tpu_custom_call" | custom-call | tf_op jit(solution)/shard_map/pallas_call | solution.py:212
  72.5 0.0 reduce-scatter.7.cloned.1.call-update
  72.6 0.0 reduce-scatter.5.cloned.1.call-start
  72.6 0.0 copy-start.1
  72.6 1.4 copy-done.1
  74.0 6.5 %shard_map.38 = bf16[16,12,2,16,128]{4,3,2,1,0:T(8,128)(2,1)S(1)} custom-call(bf16[8,4,256,768]{3,2,1,0:T(8,128)(2,1)} %get-tuple-element.8.refs_0_.refs_1_, bf16[8,4,2,16,768]{4,3,2,1,0:T(8,128)(2,1)S(1)} %copy-done.1, bf16[8,6,2,16,768]{4,3,2,1,0:T(8,128)(2,1)S(1)} %get-tuple-element.10.refs_2_.refs_3_), custom_call_target="tpu_custom_call" | custom-call | tf_op jit(solution)/shard_map/pallas_call | solution.py:179
  80.5 25.0 %all_to_all.21.f_ref = bf16[16,12,2,16,128]{4,3,2,1,0:T(8,128)(2,1)S(1)} all-to-all(bf16[16,12,2,16,128]{4,3,2,1,0:T(8,128)(2,1)S(1)} %shard_map.38), channel_id=1, replica_groups=mesh['band'=8,'lev'=16] {'lev'}, dimensions={0} | all-to-all | bytes 3145728 | tf_op jit(solution)/shard_map/all_to_all | solution.py:232
  105.5 9.6 %shard_map.39 = bf16[12,2,2,128,384]{4,3,2,1,0:T(8,128)(2,1)} custom-call(bf16[16,12,2,16,128]{4,3,2,1,0:T(8,128)(2,1)S(1)} %all_to_all.21.f_ref, bf16[12,4,2,128,384]{4,3,2,1,0:T(8,128)(2,1)} %bitcast.7), custom_call_target="tpu_custom_call" | custom-call | tf_op jit(solution)/shard_map/pallas_call | solution.py:212
  115.1 0.0 reduce-scatter.5.cloned.1.call-update
  115.1 0.0 reduce-scatter.9.cloned.1.call-start
  115.2 0.0 copy-start.2
  115.2 1.4 copy-done.2
  116.6 6.5 %shard_map.42 = bf16[16,12,2,16,128]{4,3,2,1,0:T(8,128)(2,1)S(1)} custom-call(bf16[8,4,256,768]{3,2,1,0:T(8,128)(2,1)} %get-tuple-element.8.refs_0_.refs_1_, bf16[8,4,2,16,768]{4,3,2,1,0:T(8,128)(2,1)S(1)} %copy-done.2, bf16[8,6,2,16,768]{4,3,2,1,0:T(8,128)(2,1)S(1)} %get-tuple-element.10.refs_2_.refs_3_), custom_call_target="tpu_custom_call" | custom-call | tf_op jit(solution)/shard_map/pallas_call | solution.py:179
  123.1 23.8 %all_to_all.22.f_ref = bf16[16,12,2,16,128]{4,3,2,1,0:T(8,128)(2,1)S(1)} all-to-all(bf16[16,12,2,16,128]{4,3,2,1,0:T(8,128)(2,1)S(1)} %shard_map.42), channel_id=1, replica_groups=mesh['band'=8,'lev'=16] {'lev'}, dimensions={0} | all-to-all | bytes 3145728 | tf_op jit(solution)/shard_map/all_to_all | solution.py:232
  146.9 9.7 %shard_map.43 = bf16[12,2,2,128,384]{4,3,2,1,0:T(8,128)(2,1)} custom-call(bf16[16,12,2,16,128]{4,3,2,1,0:T(8,128)(2,1)S(1)} %all_to_all.22.f_ref, bf16[12,4,2,128,384]{4,3,2,1,0:T(8,128)(2,1)} %bitcast.8), custom_call_target="tpu_custom_call" | custom-call | tf_op jit(solution)/shard_map/pallas_call | solution.py:212
  156.5 0.0 reduce-scatter.9.cloned.1.call-update
  156.6 0.0 reduce-scatter.11.cloned.1.call-start
  156.6 0.0 copy-start.3
  156.6 1.4 copy-done.3
  158.0 7.8 %shard_map.44 = bf16[16,12,2,16,128]{4,3,2,1,0:T(8,128)(2,1)S(1)} custom-call(bf16[8,4,256,768]{3,2,1,0:T(8,128)(2,1)} %get-tuple-element.8.refs_0_.refs_1_, bf16[8,4,256,768]{3,2,1,0:T(8,128)(2,1)} %get-tuple-element.8.refs_0_.refs_1_, bf16[8,4,2,16,768]{4,3,2,1,0:T(8,128)(2,1)S(1)} %copy-done.3, ...), custom_call_target="tpu_custom_call" | custom-call | tf_op jit(solution)/shard_map/pallas_call | solution.py:179
  165.8 22.4 %all_to_all.23.f_ref = bf16[16,12,2,16,128]{4,3,2,1,0:T(8,128)(2,1)S(1)} all-to-all(bf16[16,12,2,16,128]{4,3,2,1,0:T(8,128)(2,1)S(1)} %shard_map.44), channel_id=1, replica_groups=mesh['band'=8,'lev'=16] {'lev'}, dimensions={0} | all-to-all | bytes 3145728 | tf_op jit(solution)/shard_map/all_to_all | solution.py:232
  188.2 9.6 %shard_map.45 = bf16[12,2,2,128,384]{4,3,2,1,0:T(8,128)(2,1)} custom-call(bf16[16,12,2,16,128]{4,3,2,1,0:T(8,128)(2,1)S(1)} %all_to_all.23.f_ref, bf16[12,4,2,128,384]{4,3,2,1,0:T(8,128)(2,1)} %bitcast.9), custom_call_target="tpu_custom_call" | custom-call | tf_op jit(solution)/shard_map/pallas_call | solution.py:212
  197.9 0.0 reduce-scatter.11.cloned.1.call-update
  197.9 0.0 reduce-scatter.7.cloned.1.call-done
  197.9 0.0 reduce-scatter.5.cloned.1.call-done
  197.9 0.0 reduce-scatter.9.cloned.1.call-done
  198.0 36.6 %reduce-scatter.11.cloned.1.call-done = bf16[12,2,2,16,384]{4,3,2,1,0:T(8,128)(2,1)} async-done(((bf16[12,2,2,128,384]{4,3,2,1,0:T(8,128)(2,1)}), bf16[12,2,2,16,384]{4,3,2,1,0:T(8,128)(2,1)}) %reduce-scatter.11.cloned.1.call-update) | async-done | bytes 589840 | tf_op jit(solution)/shard_map/reduce_scatter | solution.py:234
  234.6 2.0 maximum_convert_fusion
  236.6 2.8 %copy.4 = f32[12,4,2,2,16,384]{5,4,3,2,1,0:T(8,128)} copy(f32[12,4,2,2,16,384]{5,4,3,2,0,1:T(8,128)S(1)} %maximum_convert_fusion) | data formatting | bytes 9437184 | tf_op jit(solution)/shard_map/convert_element_type | solution.py:236
Async XLA Ops:
  6.5 191.4 %reduce-scatter.7.cloned.1.call-start = ((), (), s32[]{:S(2)}) async-start(), calls=%async_computation.9 | async-start | bytes 5308416 | tf_op jit(solution)/shard_map/reduce_scatter | solution.py:234
  7.2 0.7 copy-start.4
  24.2 8.2 %copy-start = (bf16[8,4,2,16,768]{4,3,2,1,0:T(8,128)(2,1)}, bf16[8,4,2,16,768]{4,3,2,1,0:T(8,128)(2,1)S(1)}, u32[]{:S(2)}) copy-start(bf16[8,4,2,16,768]{4,3,2,1,0:T(8,128)(2,1)S(1)} %get-tuple-element.9.refs_1_.refs_2_) | copy-start | bytes 4718596
  72.6 125.4 %reduce-scatter.5.cloned.1.call-start = ((), (), s32[]{:S(2)}) async-start(), calls=%async_computation.8 | async-start | bytes 5308416 | tf_op jit(solution)/shard_map/reduce_scatter | solution.py:234
  72.6 1.4 copy-start.1
  115.1 82.8 %reduce-scatter.9.cloned.1.call-start = ((), (), s32[]{:S(2)}) async-start(), calls=%async_computation.10 | async-start | bytes 5308416 | tf_op jit(solution)/shard_map/reduce_scatter | solution.py:234
  115.2 1.4 copy-start.2
  156.6 78.0 %reduce-scatter.11.cloned.1.call-start = ((), (), s32[]{:S(2)}) async-start(), calls=%async_computation.11 | async-start | bytes 5308416 | tf_op jit(solution)/shard_map/reduce_scatter | solution.py:234
  156.6 1.4 copy-start.3
Sparse Core Ops, SparseCore 0:
  72.7 36.9 reduce-scatter.6
  115.3 37.0 reduce-scatter.4
  156.7 36.9 reduce-scatter.8
  198.0 36.5 reduce-scatter.10

commit v2 on v1

--- a/solution.py
+++ b/solution.py
@@ -12,6 +12,8 @@
 COS = (1.0, -19.73920440673828, 64.9390869140625, -85.4496078491211, 60.16310119628906, -25.950063705444336, 6.50340461730957)
 SIN = (6.283182621002197, -41.341392517089844, 81.59541320800781, -76.57229614257812, 41.17121124267578, -12.217327117919922)
 LANES = 128
+ROWS = 4
+MESH = pl.DeviceIdType.MESH
 
 
 def poly(coefs, z):
@@ -118,49 +120,43 @@
     )(lon_counts, 1.0 / lon_counts.astype(F32), grid_values)
 
 
-def transform_kernel(u, *refs):
-    if u % 2:
-        a_ref, b_ref, coarse_ref, fine_ref, out_ref, table, total = refs
-        sources = (a_ref, b_ref)
-    else:
-        a_ref, coarse_ref, fine_ref, out_ref, table, total = refs
-        sources = (a_ref,)
-    pair = pl.program_id(0)
-    pairs = pl.num_programs(0)
+def transform_kernel(a_ref, b_ref, coarse_ref, fine_ref, out_ref, table, total):
+    u = pl.program_id(0)
+    pair = pl.program_id(1)
+    pairs = pl.num_programs(1)
     halves = fine_ref.shape[0]
     owners = coarse_ref.shape[1]
+    fields = out_ref.shape[-1]
     for step in range(halves):
         for j, (k, l) in enumerate(((0, 0), (1, 0), (0, 1), (1, 1))):
             table[pl.ds((4 * step + j) * owners, owners), :] = coarse_ref[k] * fine_ref[step, l]
-    sums = [
-        lax.dot_general(table[...], ref[...], (((1,), (1,)), ((), ())), preferred_element_type=F32)
-        for ref in sources
-    ]
     spot = pl.ds(pair, owners, stride=8)
-    fields = out_ref.shape[-1]
 
     def keep(t, real, imag):
         for r, value in enumerate((real, imag)):
             for s in range(2):
                 total[4 * t + 2 * r + s, spot, :] = value[:, s * fields : (s + 1) * fields]
 
-    for step in range(halves):
-        waves = []
-        for part in sums:
+    def waves(ref):
+        part = lax.dot_general(table[...], ref[...], (((1,), (1,)), ((), ())), preferred_element_type=F32)
+        out = []
+        for step in range(halves):
             cc, sc, cs, ss = (part[(4 * step + j) * owners : (4 * step + j + 1) * owners] for j in range(4))
-            waves.append((cc - ss, sc + cs, cc + ss, sc - cs))
-        if u % 2:
-            (ca, sa, da, ta), (cb, sb, db, tb) = waves
-            if u == 1:
-                keep(halves + step, ca - sb, -(sa + cb))
-                keep(halves - 1 - step, da - tb, -(ta + db))
-            else:
-                keep(halves + step, ca + sb, cb - sa)
-                keep(halves - 1 - step, da + tb, db - ta)
-        else:
-            ((ca, sa, da, ta),) = waves
+            out.append((cc - ss, sc + cs, cc + ss, sc - cs))
+        return out
+
+    @pl.when(u % 2 == 0)
+    def _():
+        for step, (ca, sa, da, ta) in enumerate(waves(a_ref)):
             keep(halves + step, ca, -sa)
             keep(halves - 1 - step, da, -ta)
+
+    @pl.when(u % 2 == 1)
+    def _():
+        sign = jnp.where(u == 1, 1.0, -1.0).astype(F32)
+        for step, ((ca, sa, da, ta), (cb, sb, db, tb)) in enumerate(zip(waves(a_ref), waves(b_ref))):
+            keep(halves + step, ca - sign * sb, -(sa + sign * cb))
+            keep(halves - 1 - step, da - sign * tb, -(ta + sign * db))
 
     @pl.when(pair == pairs - 1)
     def _():
@@ -171,69 +167,300 @@
                 out_ref[:, t, s] = jnp.concatenate([real, imag], axis=1).astype(BF16)
 
 
-def transform(u, y, coarse, fine):
+def transform(y, coarse, fine):
     pairs, _, columns, width = y.shape
     halves, _, owners = fine.shape[1:4]
     fields = columns // 2
-    used = (1, 3) if u % 2 else (u,)
     return pl.pallas_call(
-        functools.partial(transform_kernel, u),
-        grid=(pairs,),
-        out_shape=jax.ShapeDtypeStruct((owners, 2 * halves, 2, 2 * pairs, fields), BF16),
-        in_specs=[pl.BlockSpec((None, None, columns, width), functools.partial(lambda k, p: (p, k, 0, 0), k)) for k in used]
-        + [
-            pl.BlockSpec((None, None, 2, owners, width), lambda p: (p, u, 0, 0, 0)),
-            pl.BlockSpec((None, halves, 2, owners, width), lambda p: (p, 0, 0, 0, 0)),
+        transform_kernel,
+        grid=(4, pairs),
+        out_shape=jax.ShapeDtypeStruct((4, owners, 2 * halves, 2, 2 * pairs, fields), BF16),
+        in_specs=[
+            pl.BlockSpec((None, None, columns, width), lambda u, p: (p, u - u // 3 * 2, 0, 0)),
+            pl.BlockSpec((None, None, columns, width), lambda u, p: (p * (u % 2), 3, 0, 0)),
+            pl.BlockSpec((None, None, 2, owners, width), lambda u, p: (p, u, 0, 0, 0)),
+            pl.BlockSpec((None, halves, 2, owners, width), lambda u, p: (p, 0, 0, 0, 0)),
         ],
-        out_specs=pl.BlockSpec((owners, 2 * halves, 2, 2 * pairs, fields), lambda p: (0, 0, 0, 0, 0)),
+        out_specs=pl.BlockSpec((None, owners, 2 * halves, 2, 2 * pairs, fields), lambda u, p: (u, 0, 0, 0, 0, 0)),
         scratch_shapes=[
             pltpu.VMEM((4 * halves * owners, width), BF16),
             pltpu.VMEM((8 * halves, owners * pairs, fields), F32),
         ],
         compiler_params=pltpu.CompilerParams(vmem_limit_bytes=48 * 2**20),
-    )(*[y] * len(used), coarse, fine)
-
-
-def legendre_kernel(f_ref, l_ref, out_ref):
-    owners, _, both, fields = f_ref.shape
+    )(y, y, coarse, fine)
+
+
+def exchange_kernel(
+    chunk, ahead, folded, legendre, out, inbox, weights, partial, from_core, first_out, from_first, second_out, from_second, staged,
+    send_sem, recv_sem, weight_sem, core_send, core_recv, first_send, first_recv, second_send, second_recv, out_sem,
+):
+    _, owners, groups, _, both, fields = folded.shape
+    degrees = legendre.shape[-1]
     pairs = both // 2
-    for s in range(2):
-        f = f_ref[:, s].astype(F32).reshape(owners, 2, pairs, fields)
-        for r in range(2):
-            part = f[:, r].reshape(owners * pairs, fields).astype(BF16)
-            out_ref[s, r] = lax.dot_general(
-                part, l_ref[s], (((0,), (0,)), ((), ())), preferred_element_type=F32
-            ).astype(BF16)
-
-
-def legendre_sums(u, folded, legendre):
-    owners, groups, _, both, fields = folded.shape
+    per_class = groups // chunk
+    chunks = 4 * per_class
+    half = 2 * chunk
+    block = fields // 8
+    band, lev = lax.axis_index("band"), lax.axis_index("lev")
+    chip, core = band // 2, band % 2
+    beside = chip + 1 - 2 * (chip % 2)
+    facing = 3 - chip
+    opposite = (chip + 2) % 4
+    first, second = (beside, facing), (facing, beside)
+    sibling = {"band": chip * 2 + 1 - core}
+
+    def on_chip(c):
+        return {"band": c * 2 + core}
+
+    def owner(d):
+        return {"lev": d}
+
+    def place(c):
+        return c // per_class, pl.ds(c % per_class * chunk, chunk)
+
+    barrier = pltpu.get_barrier_semaphore()
+    for j in range(1, owners):
+        pl.semaphore_signal(barrier, inc=1, device_id=owner((lev + j) % owners), device_id_type=MESH)
+    for device in (sibling, on_chip(beside), on_chip(facing)):
+        pl.semaphore_signal(barrier, inc=1, device_id=device, device_id_type=MESH)
+    pl.semaphore_wait(barrier, owners + 2)
+
+    def to_owner(c, d):
+        u, t = place(c)
+        return pltpu.make_async_remote_copy(
+            src_ref=folded.at[u, d, t],
+            dst_ref=inbox.at[c, lev],
+            send_sem=send_sem.at[c, d],
+            recv_sem=recv_sem.at[c, lev],
+            device_id=owner(d),
+            device_id_type=MESH,
+        )
+
+    def from_owner(c, d):
+        u, t = place(c)
+        return pltpu.make_async_remote_copy(
+            src_ref=folded.at[u, d, t],
+            dst_ref=inbox.at[c, d],
+            send_sem=send_sem.at[c, d],
+            recv_sem=recv_sem.at[c, d],
+            device_id=owner(d),
+            device_id_type=MESH,
+        )
+
+    def own(c):
+        u, t = place(c)
+        return pltpu.make_async_copy(folded.at[u, lev, t], inbox.at[c, lev], recv_sem.at[c, lev])
+
+    def weight(c):
+        u, t = place(c)
+        return pltpu.make_async_copy(legendre.at[t, u], weights.at[c], weight_sem.at[c])
+
+    def across(c):
+        return pltpu.make_async_remote_copy(
+            src_ref=partial.at[c % 4, 1 - core],
+            dst_ref=from_core.at[c],
+            send_sem=core_send.at[c],
+            recv_sem=core_recv.at[c],
+            device_id=sibling,
+            device_id_type=MESH,
+        )
+
+    def first_step(c, v):
+        return pltpu.make_async_remote_copy(
+            src_ref=first_out.at[c % 2, v],
+            dst_ref=from_first.at[c, v],
+            send_sem=first_send.at[c, v],
+            recv_sem=first_recv.at[c, v],
+            device_id=on_chip(first[v]),
+            device_id_type=MESH,
+        )
+
+    def second_step(c, v):
+        return pltpu.make_async_remote_copy(
+            src_ref=second_out.at[c % 2, v],
+            dst_ref=from_second.at[c, v],
+            send_sem=second_send.at[c, v],
+            recv_sem=second_recv.at[c, v],
+            device_id=on_chip(second[v]),
+            device_id_type=MESH,
+        )
+
+    def result(c):
+        u, t = place(c)
+        return pltpu.make_async_copy(staged.at[c % 2], out.at[t, u], out_sem.at[c])
+
+    def launch(c):
+        own(c).start()
+        weight(c).start()
+
+        def one(j, carry):
+            to_owner(c, (lev + j) % owners).start()
+            return carry
+
+        lax.fori_loop(1, owners, one, 0)
+
+    def sums(c):
+        own(c).wait()
+        weight(c).wait()
+
+        def one(j, carry):
+            from_owner(c, (lev + j) % owners).wait_recv()
+            to_owner(c, (lev + j) % owners).wait_send()
+            return carry
+
+        lax.fori_loop(1, owners, one, 0)
+
+        def wave(t, carry):
+            for s in range(2):
+                f = inbox[c, :, t, s].astype(F32).reshape(owners, 2, pairs, fields)
+                part = jnp.concatenate(
+                    [f[:, r].reshape(owners * pairs, fields) for r in range(2)], axis=1
+                ).astype(BF16)
+                total = lax.dot_general(
+                    part, weights[c, t, s], (((0,), (0,)), ((), ())), preferred_element_type=F32
+                ).astype(BF16)
+                for r in range(2):
+                    for b in range(8):
+                        at = r * fields + b * block
+                        partial[c % 4, b % 2, b // 2, 4 * t + 2 * s + r] = total[at : at + block]
+            return carry
+
+        lax.fori_loop(0, chunk, wave, 0)
+        across(c).start()
+
+    def parts(c, v, row, target):
+        at = pl.ds(v * half + row, ROWS)
+        return partial[c % 4, core, target, at].astype(F32) + from_core[c, target, at].astype(F32)
+
+    def rows(body):
+        def one(i, carry):
+            body(i * ROWS)
+            return carry
+
+        lax.fori_loop(0, half // ROWS, one, 0)
+
+    def first_stage(c):
+        across(c).wait()
+        for v in range(2):
+
+            def add(row):
+                for w, target in enumerate((first[v], opposite)):
+                    first_out[c % 2, v, w, pl.ds(row, ROWS)] = parts(c, v, row, target).astype(BF16)
+
+            rows(add)
+            first_step(c, v).start()
+
+    def second_stage(c):
+        for v in range(2):
+            first_step(c, v).wait()
+
+            def add(row):
+                at = pl.ds(row, ROWS)
+                both = parts(c, v, row, second[v]) + from_first[c, v, 1, at].astype(F32)
+                second_out[c % 2, v, at] = both.astype(BF16)
+
+            rows(add)
+            second_step(c, v).start()
+
+    def last_stage(c):
+        @pl.when(c >= 2)
+        def _():
+            result(c - 2).wait()
+
+        for v in range(2):
+            second_step(c, v).wait()
+
+            def add(row):
+                at = pl.ds(row, ROWS)
+                both = parts(c, v, row, chip) + from_first[c, v, 0, at].astype(F32) + from_second[c, v, at].astype(F32)
+                for i in range(ROWS // 4):
+                    staged[c % 2, v * (chunk // 2) + row // 4 + i] = both[4 * i : 4 * i + 4].astype(BF16)
+
+            rows(add)
+        result(c).start()
+
+    for c in range(ahead):
+        launch(c)
+
+    def turn(c, carry):
+        @pl.when(c + ahead < chunks)
+        def _():
+            launch(c + ahead)
+
+        @pl.when(c < chunks)
+        def _():
+            sums(c)
+
+        @pl.when((c >= 1) & (c <= chunks))
+        def _():
+            first_stage(c - 1)
+
+        @pl.when((c >= 2) & (c <= chunks + 1))
+        def _():
+            second_stage(c - 2)
+
+        @pl.when(c >= 3)
+        def _():
+            last_stage(c - 3)
+
+        return carry
+
+    lax.fori_loop(0, chunks + 3, turn, 0)
+    result(chunks - 2).wait()
+    result(chunks - 1).wait()
+
+
+def exchange(folded, legendre, chunk, ahead):
+    _, owners, groups, _, both, fields = folded.shape
     _, _, _, latitudes, degrees = legendre.shape
+    chunks = 4 * groups // chunk
+    half = 2 * chunk
+    block = fields // 8
+    dma = pltpu.SemaphoreType.DMA
+    anywhere = pl.BlockSpec(memory_space=pl.ANY)
     return pl.pallas_call(
-        legendre_kernel,
-        grid=(groups,),
-        out_shape=jax.ShapeDtypeStruct((groups, 2, 2, fields, degrees), BF16),
-        in_specs=[
-            pl.BlockSpec((owners, None, 2, both, fields), lambda k: (0, k, 0, 0, 0)),
-            pl.BlockSpec((None, None, 2, latitudes, degrees), lambda k: (k, u, 0, 0, 0)),
+        functools.partial(exchange_kernel, chunk, ahead),
+        out_shape=jax.ShapeDtypeStruct((groups, 4, 4, block, degrees), BF16),
+        in_specs=[anywhere, anywhere],
+        out_specs=anywhere,
+        scratch_shapes=[
+            pltpu.VMEM((chunks, owners, chunk, 2, both, fields), BF16),
+            pltpu.VMEM((chunks, chunk, 2, latitudes, degrees), BF16),
+            pltpu.VMEM((4, 2, 4, 2 * half, block, degrees), BF16),
+            pltpu.VMEM((chunks, 4, 2 * half, block, degrees), BF16),
+            pltpu.VMEM((2, 2, 2, half, block, degrees), BF16),
+            pltpu.VMEM((chunks, 2, 2, half, block, degrees), BF16),
+            pltpu.VMEM((2, 2, half, block, degrees), BF16),
+            pltpu.VMEM((chunks, 2, half, block, degrees), BF16),
+            pltpu.VMEM((2, chunk, 4, block, degrees), BF16),
+            dma((chunks, owners)),
+            dma((chunks, owners)),
+            dma((chunks,)),
+            dma((chunks,)),
+            dma((chunks,)),
+            dma((chunks, 2)),
+            dma((chunks, 2)),
+            dma((chunks, 2)),
+            dma((chunks, 2)),
+            dma((chunks,)),
         ],
-        out_specs=pl.BlockSpec((None, 2, 2, fields, degrees), lambda k: (k, 0, 0, 0, 0)),
-        compiler_params=pltpu.CompilerParams(vmem_limit_bytes=48 * 2**20),
+        compiler_params=pltpu.CompilerParams(
+            collective_id=0, has_side_effects=True, vmem_limit_bytes=60 * 2**20
+        ),
     )(folded, legendre)
+
+
+CHUNK = 6
+AHEAD = 2
 
 
 def on_device(owners, grid_values, lon_counts, legendre):
     owned = legendre.shape[0]
     y, coarse, fine = prepare(grid_values, lon_counts, owners, owned)
+    folded = transform(y, coarse, fine)
     by_class = legendre.reshape(owned // 4, 4, *legendre.shape[1:])
-    results = []
-    for u in range(4):
-        chunk = transform(u, y, coarse, fine)
-        folded = lax.all_to_all(chunk, "lev", split_axis=0, concat_axis=0, tiled=True)
-        partial_sums = legendre_sums(u, folded, by_class)
-        results.append(lax.psum_scatter(partial_sums, "band", scatter_dimension=3, tiled=True))
-    spectra = jnp.stack(results, axis=1)
-    return spectra.reshape(owned, *spectra.shape[2:]).astype(F32)
+    spectra = exchange(folded, by_class, CHUNK, AHEAD)
+    return spectra.reshape(owned, 2, 2, *spectra.shape[3:]).astype(F32)
 
 
 def solution(mesh):

time: 248 us -> 171 us (0.69)
  blocking collectives: 102 us -> 0 us
  Pallas kernels: 83.8 us -> 164 us
  waiting for transfers between devices: 36.8 us -> 0 us
  between operations: 13.2 us -> 0.01 us
  local copies, waits for them, and re-layouts: 7.7 us -> 0.66 us
  other arithmetic: 2.66 us -> 5.15 us
    all_to_all x4 -> x0, blocking collectives: 102 us -> none  [on_device(): lax.all_to_all(chunk, 'lev', split_axis=0, concat_axis=0, tiled=True)]
    pallas_call x8 -> x2, Pallas kernels: 67.5 us -> 148 us  [the longest x1 117 us: exchange(): pl.pallas_call(functools.partial(exchange_kernel, chunk, ahead), out_shap...]
    reduce_scatter x4 -> x0, waiting for transfers between devices: 36.7 us -> none  [on_device(): lax.psum_scatter(partial_sums, 'band', scatter_dimension=3, tiled=True)]
    unnamed x10 -> x2, local copies, waits for them, and re-layouts: 4.87 us -> 0.66 us
    convert_element_type x1 -> x0, local copies, waits for them, and re-layouts: 2.83 us -> none  [on_device(): return spectra.reshape(owned, *spectra.shape[2:]).astype(F32)]
    convert_element_type x1, other arithmetic: 2 us -> 4.5 us  [on_device(): return spectra.reshape(owned, 2, 2, *spectra.shape[3:]).astype(F32)]
  transfers between devices with their start and end apart: 4 -> 0, of which waited for: 1 -> 0; matrix products, arithmetic and copies ran while one was open for 0% -> 0% of each run, Pallas kernels for 20% -> 0%
where the time goes in v2:
time: 171 us; the launch traced here: 170 us
  Pallas kernels  164 us (96%)
  other arithmetic  5.15 us (3%)
    pallas_call x1, Pallas kernels, exchange(): pl.pallas_call(functools.partial(exchange_kernel, chunk, ahead), out_shap...  117 us
    pallas_call x1, Pallas kernels, transform(): pl.pallas_call(transform_kernel, grid=(4, pairs), out_shape=jax.ShapeDtyp...  30.3 us
    pallas_call x1, Pallas kernels, prepare(): pl.pallas_call(functools.partial(prepare_kernel, owners, owned), grid=(pa...  16.3 us
    convert_element_type x1, other arithmetic, on_device(): return spectra.reshape(owned, 2, 2, *spectra.shape[3:]).astype(F32)  4.5 us

profile of v2, /device:TPU:0, one launch (start us, length us, event | category | flops | bytes accessed | tf_op | source)
XLA Modules:
  0.0 169.9 jit_solution(7815417287334169611)
XLA Ops:
  0.0 0.7 convert_divide_fusion.inverse_ref
  0.7 0.0 copy-start
  0.7 0.7 copy-done
  1.3 16.3 %shard_map.37 = (bf16[8,4,256,768]{3,2,1,0:T(8,128)(2,1)}, bf16[8,4,2,16,768]{4,3,2,1,0:T(8,128)(2,1)S(1)}, bf16[8,6,2,16,768]{4,3,2,1,0:T(8,128)(2,1)S(1)}) custom-call(s32[8]{0:T(128)S(1)} %copy-done, f32[8]{0:T(128)S(1)} %convert_divide_fusion.inverse_ref, bf16[8,2,128,3072]{3,2,1,0:T(8,128)(2,1)} %x_ref.1), custom_call_target="tpu_custom_call" | custom-call | tf_op jit(solution)/shard_map/pallas_call | solution.py:105
  17.6 30.3 %shard_map.38.folded = bf16[4,16,12,2,16,128]{5,4,3,2,1,0:T(8,128)(2,1)} custom-call(bf16[8,4,256,768]{3,2,1,0:T(8,128)(2,1)} %get-tuple-element.8.a_ref.b_ref, bf16[8,4,256,768]{3,2,1,0:T(8,128)(2,1)} %get-tuple-element.8.a_ref.b_ref, bf16[8,4,2,16,768]{4,3,2,1,0:T(8,128)(2,1)S(1)} %get-tuple-element.9.coarse_ref, ...), custom_call_target="tpu_custom_call" | custom-call | tf_op jit(solution)/shard_map/pallas_call | solution.py:174
  48.0 117.4 %shard_map.39 = bf16[12,4,4,16,384]{4,3,2,1,0:T(8,128)(2,1)} custom-call(bf16[4,16,12,2,16,128]{5,4,3,2,1,0:T(8,128)(2,1)} %shard_map.38.folded, bf16[12,4,2,128,384]{4,3,2,1,0:T(8,128)(2,1)} %bitcast.4), custom_call_target="tpu_custom_call" | custom-call | tf_op jit(solution)/shard_map/pallas_call | solution.py:421
  165.4 4.5 %convert.1 = f32[48,2,2,16,384]{4,3,2,1,0:T(8,128)} convert(bf16[48,2,2,16,384]{4,3,2,1,0:T(8,128)(2,1)} %bitcast.3) | non-fusion elementwise | flops 1179648 | bytes 7077888 | tf_op jit(solution)/shard_map/convert_element_type | solution.py:463
Async XLA Ops:
  0.7 0.7 copy-start

commit v3 on v2

--- a/solution.py
+++ b/solution.py
@@ -69,7 +69,9 @@
             to = pl.ds(pl.multiple_of(step * rows + s * fields, rows), rows)
             for i in range(tiles):
                 inside = lane + i * LANES < quarter
-                x0, x1, x2, x3 = (jnp.where(inside, pieces[k][s][i], 0.0) for k in range(4))
+                x0, x1, x2, x3 = (pieces[k][s][i] for k in range(4))
+                if (i + 1) * LANES > points // 8:
+                    x0, x1, x2, x3 = (jnp.where(inside, x, 0.0) for x in (x0, x1, x2, x3))
                 at = pl.ds(i * LANES, LANES)
                 y_ref[0, to, at] = ((x0 + x2) + (x1 + x3)).astype(BF16)
                 y_ref[1, to, at] = (x0 - x2).astype(BF16)
@@ -85,14 +87,15 @@
     middle = 2 * groups - 2
     place = lax.broadcasted_iota(jnp.int32, (16, width), 1).astype(F32)
     row = lax.broadcasted_iota(jnp.int32, (16, width), 0).astype(F32)
+    rates = jnp.where(row < 8, 4 * row + 2, row + float(middle - 8))
+    near_cos, near_sin = cos_sin(place * rates, n, inverse)
     for step in range(groups // 2):
-        c, s = cos_sin(place * float(4 * step + 2), n, inverse)
-        fine_ref[step, 0] = c.astype(BF16)
-        fine_ref[step, 1] = s.astype(BF16)
+        for r, near in enumerate((near_cos, near_sin)):
+            fine_ref[step, r] = jnp.broadcast_to(near[step : step + 1], (16, width)).astype(BF16)
     owner_cos, owner_sin = cos_sin(place * (row * float(owned)), n, inverse)
     owner_cos, owner_sin = owner_cos * inverse, owner_sin * inverse
     for u in range(4):
-        c, s = cos_sin(place * float(middle + u), n, inverse)
+        c, s = near_cos[8 + u : 9 + u], near_sin[8 + u : 9 + u]
         coarse_ref[u, 0] = (owner_cos * c - owner_sin * s).astype(BF16)
         coarse_ref[u, 1] = (owner_sin * c + owner_cos * s).astype(BF16)
 
@@ -120,79 +123,10 @@
     )(lon_counts, 1.0 / lon_counts.astype(F32), grid_values)
 
 
-def transform_kernel(a_ref, b_ref, coarse_ref, fine_ref, out_ref, table, total):
-    u = pl.program_id(0)
-    pair = pl.program_id(1)
-    pairs = pl.num_programs(1)
-    halves = fine_ref.shape[0]
-    owners = coarse_ref.shape[1]
-    fields = out_ref.shape[-1]
-    for step in range(halves):
-        for j, (k, l) in enumerate(((0, 0), (1, 0), (0, 1), (1, 1))):
-            table[pl.ds((4 * step + j) * owners, owners), :] = coarse_ref[k] * fine_ref[step, l]
-    spot = pl.ds(pair, owners, stride=8)
-
-    def keep(t, real, imag):
-        for r, value in enumerate((real, imag)):
-            for s in range(2):
-                total[4 * t + 2 * r + s, spot, :] = value[:, s * fields : (s + 1) * fields]
-
-    def waves(ref):
-        part = lax.dot_general(table[...], ref[...], (((1,), (1,)), ((), ())), preferred_element_type=F32)
-        out = []
-        for step in range(halves):
-            cc, sc, cs, ss = (part[(4 * step + j) * owners : (4 * step + j + 1) * owners] for j in range(4))
-            out.append((cc - ss, sc + cs, cc + ss, sc - cs))
-        return out
-
-    @pl.when(u % 2 == 0)
-    def _():
-        for step, (ca, sa, da, ta) in enumerate(waves(a_ref)):
-            keep(halves + step, ca, -sa)
-            keep(halves - 1 - step, da, -ta)
-
-    @pl.when(u % 2 == 1)
-    def _():
-        sign = jnp.where(u == 1, 1.0, -1.0).astype(F32)
-        for step, ((ca, sa, da, ta), (cb, sb, db, tb)) in enumerate(zip(waves(a_ref), waves(b_ref))):
-            keep(halves + step, ca - sign * sb, -(sa + sign * cb))
-            keep(halves - 1 - step, da - sign * tb, -(ta + sign * db))
-
-    @pl.when(pair == pairs - 1)
-    def _():
-        for t in range(2 * halves):
-            for s in range(2):
-                real = total[4 * t + s].reshape(owners, 8, fields)
-                imag = total[4 * t + 2 + s].reshape(owners, 8, fields)
-                out_ref[:, t, s] = jnp.concatenate([real, imag], axis=1).astype(BF16)
-
-
-def transform(y, coarse, fine):
-    pairs, _, columns, width = y.shape
-    halves, _, owners = fine.shape[1:4]
-    fields = columns // 2
-    return pl.pallas_call(
-        transform_kernel,
-        grid=(4, pairs),
-        out_shape=jax.ShapeDtypeStruct((4, owners, 2 * halves, 2, 2 * pairs, fields), BF16),
-        in_specs=[
-            pl.BlockSpec((None, None, columns, width), lambda u, p: (p, u - u // 3 * 2, 0, 0)),
-            pl.BlockSpec((None, None, columns, width), lambda u, p: (p * (u % 2), 3, 0, 0)),
-            pl.BlockSpec((None, None, 2, owners, width), lambda u, p: (p, u, 0, 0, 0)),
-            pl.BlockSpec((None, halves, 2, owners, width), lambda u, p: (p, 0, 0, 0, 0)),
-        ],
-        out_specs=pl.BlockSpec((None, owners, 2 * halves, 2, 2 * pairs, fields), lambda u, p: (u, 0, 0, 0, 0, 0)),
-        scratch_shapes=[
-            pltpu.VMEM((4 * halves * owners, width), BF16),
-            pltpu.VMEM((8 * halves, owners * pairs, fields), F32),
-        ],
-        compiler_params=pltpu.CompilerParams(vmem_limit_bytes=48 * 2**20),
-    )(y, y, coarse, fine)
-
-
 def exchange_kernel(
-    chunk, ahead, folded, legendre, out, inbox, weights, partial, from_core, first_out, from_first, second_out, from_second, staged,
-    send_sem, recv_sem, weight_sem, core_send, core_recv, first_send, first_recv, second_send, second_recv, out_sem,
+    chunk, ahead, coarse, fine, y, legendre, out,
+    samples, table, total, folded, inbox, weights, partial, from_core, first_out, from_first, second_out, from_second, staged,
+    sample_sem, send_sem, recv_sem, weight_sem, core_send, core_recv, first_send, first_recv, second_send, second_recv, out_sem,
 ):
     _, owners, groups, _, both, fields = folded.shape
     degrees = legendre.shape[-1]
@@ -218,6 +152,85 @@
     def place(c):
         return c // per_class, pl.ds(c % per_class * chunk, chunk)
 
+    count = y.shape[0]
+    halves = groups // 2
+
+    def sample(g, part):
+        u, p = g // count, g % count
+        kind = 3 if part else u - u // 3 * 2
+        return pltpu.make_async_copy(y.at[p, kind], samples.at[g % 2, part], sample_sem.at[g % 2, part])
+
+    def fetch(g):
+        sample(g, 0).start()
+
+        @pl.when(g // count % 2 == 1)
+        def _():
+            sample(g, 1).start()
+
+    def transform(g):
+        u, p = g // count, g % count
+
+        @pl.when(g + 1 < 4 * count)
+        def _():
+            fetch(g + 1)
+
+        for step in range(halves):
+            for j, (k, l) in enumerate(((0, 0), (1, 0), (0, 1), (1, 1))):
+                table[pl.ds((4 * step + j) * owners, owners), :] = coarse[p, u, k] * fine[p, step, l]
+        spot = pl.ds(p, owners, stride=8)
+
+        def keep(t, real, imag):
+            for r, value in enumerate((real, imag)):
+                for s in range(2):
+                    total[4 * t + 2 * r + s, spot, :] = value[:, s * fields : (s + 1) * fields]
+
+        def waves(part):
+            sums = lax.dot_general(
+                table[...], samples[g % 2, part], (((1,), (1,)), ((), ())), preferred_element_type=F32
+            )
+            found = []
+            for step in range(halves):
+                cc, sc, cs, ss = (sums[(4 * step + j) * owners : (4 * step + j + 1) * owners] for j in range(4))
+                found.append((cc - ss, sc + cs, cc + ss, sc - cs))
+            return found
+
+        sample(g, 0).wait()
+
+        @pl.when(u % 2 == 0)
+        def _():
+            for step, (ca, sa, da, ta) in enumerate(waves(0)):
+                keep(halves + step, ca, -sa)
+                keep(halves - 1 - step, da, -ta)
+
+        @pl.when(u % 2 == 1)
+        def _():
+            sample(g, 1).wait()
+            sign = (2 - u).astype(F32)
+            for step, ((ca, sa, da, ta), (cb, sb, db, tb)) in enumerate(zip(waves(0), waves(1))):
+                keep(halves + step, ca - sign * sb, -(sa + sign * cb))
+                keep(halves - 1 - step, da - sign * tb, -(ta + sign * db))
+
+        @pl.when(p == count - 1)
+        def _():
+            def pack(t, carry):
+                for s in range(2):
+                    real = total[4 * t + s].reshape(owners, pairs, fields)
+                    imag = total[4 * t + 2 + s].reshape(owners, pairs, fields)
+                    folded[u, :, t, s] = jnp.concatenate([real, imag], axis=1).astype(BF16)
+                return carry
+
+            lax.fori_loop(0, groups, pack, 0)
+
+    def transform_part(q):
+        u, i = q // per_class, q % per_class
+
+        def one(p, carry):
+            transform(u * count + p)
+            return carry
+
+        lax.fori_loop(i * count // per_class, (i + 1) * count // per_class, one, 0)
+
+    fetch(0)
     barrier = pltpu.get_barrier_semaphore()
     for j in range(1, owners):
         pl.semaphore_signal(barrier, inc=1, device_id=owner((lev + j) % owners), device_id_type=MESH)
@@ -253,7 +266,7 @@
 
     def weight(c):
         u, t = place(c)
-        return pltpu.make_async_copy(legendre.at[t, u], weights.at[c], weight_sem.at[c])
+        return pltpu.make_async_copy(legendre.at[t, u], weights.at[c % (ahead + 1)], weight_sem.at[c])
 
     def across(c):
         return pltpu.make_async_remote_copy(
@@ -317,7 +330,7 @@
                     [f[:, r].reshape(owners * pairs, fields) for r in range(2)], axis=1
                 ).astype(BF16)
                 total = lax.dot_general(
-                    part, weights[c, t, s], (((0,), (0,)), ((), ())), preferred_element_type=F32
+                    part, weights[c % (ahead + 1), t, s], (((0,), (0,)), ((), ())), preferred_element_type=F32
                 ).astype(BF16)
                 for r in range(2):
                     for b in range(8):
@@ -379,10 +392,18 @@
             rows(add)
         result(c).start()
 
+    for q in range(per_class):
+        transform_part(q)
     for c in range(ahead):
         launch(c)
+    for q in range(per_class, per_class + ahead - 1):
+        transform_part(q)
 
     def turn(c, carry):
+        @pl.when(c + ahead + per_class - 1 < chunks)
+        def _():
+            transform_part(c + ahead + per_class - 1)
+
         @pl.when(c + ahead < chunks)
         def _():
             launch(c + ahead)
@@ -410,22 +431,28 @@
     result(chunks - 1).wait()
 
 
-def exchange(folded, legendre, chunk, ahead):
-    _, owners, groups, _, both, fields = folded.shape
-    _, _, _, latitudes, degrees = legendre.shape
+def exchange(y, coarse, fine, legendre, chunk, ahead):
+    count, _, columns, width = y.shape
+    owners, fields, both = coarse.shape[3], columns // 2, 2 * count
+    groups, _, _, latitudes, degrees = legendre.shape
     chunks = 4 * groups // chunk
     half = 2 * chunk
     block = fields // 8
     dma = pltpu.SemaphoreType.DMA
     anywhere = pl.BlockSpec(memory_space=pl.ANY)
+    inside = pl.BlockSpec(memory_space=pltpu.VMEM)
     return pl.pallas_call(
         functools.partial(exchange_kernel, chunk, ahead),
         out_shape=jax.ShapeDtypeStruct((groups, 4, 4, block, degrees), BF16),
-        in_specs=[anywhere, anywhere],
+        in_specs=[inside, inside, anywhere, anywhere],
         out_specs=anywhere,
         scratch_shapes=[
+            pltpu.VMEM((2, 2, columns, width), BF16),
+            pltpu.VMEM((2 * groups * owners, width), BF16),
+            pltpu.VMEM((4 * groups, owners * count, fields), F32),
+            pltpu.VMEM((4, owners, groups, 2, both, fields), BF16),
             pltpu.VMEM((chunks, owners, chunk, 2, both, fields), BF16),
-            pltpu.VMEM((chunks, chunk, 2, latitudes, degrees), BF16),
+            pltpu.VMEM((ahead + 1, chunk, 2, latitudes, degrees), BF16),
             pltpu.VMEM((4, 2, 4, 2 * half, block, degrees), BF16),
             pltpu.VMEM((chunks, 4, 2 * half, block, degrees), BF16),
             pltpu.VMEM((2, 2, 2, half, block, degrees), BF16),
@@ -433,6 +460,7 @@
             pltpu.VMEM((2, 2, half, block, degrees), BF16),
             pltpu.VMEM((chunks, 2, half, block, degrees), BF16),
             pltpu.VMEM((2, chunk, 4, block, degrees), BF16),
+            dma((2, 2)),
             dma((chunks, owners)),
             dma((chunks, owners)),
             dma((chunks,)),
@@ -447,19 +475,18 @@
         compiler_params=pltpu.CompilerParams(
             collective_id=0, has_side_effects=True, vmem_limit_bytes=60 * 2**20
         ),
-    )(folded, legendre)
-
-
-CHUNK = 6
+    )(coarse, fine, y, legendre)
+
+
+CHUNK = 4
 AHEAD = 2
 
 
 def on_device(owners, grid_values, lon_counts, legendre):
     owned = legendre.shape[0]
     y, coarse, fine = prepare(grid_values, lon_counts, owners, owned)
-    folded = transform(y, coarse, fine)
     by_class = legendre.reshape(owned // 4, 4, *legendre.shape[1:])
-    spectra = exchange(folded, by_class, CHUNK, AHEAD)
+    spectra = exchange(y, coarse, fine, by_class, CHUNK, AHEAD)
     return spectra.reshape(owned, 2, 2, *spectra.shape[3:]).astype(F32)
 
 

time: 171 us -> 145 us (0.85)
  Pallas kernels: 164 us -> 135 us
  local copies, waits for them, and re-layouts: 0.66 us -> 3.22 us
    pallas_call x1 -> x0, Pallas kernels: 30.3 us -> none  [transform(): pl.pallas_call(transform_kernel, grid=(4, pairs), out_shape=jax.ShapeDtyp...]
    unnamed x2 -> x6, local copies, waits for them, and re-layouts: 0.66 us -> 3.22 us
    pallas_call x1, Pallas kernels: 117 us -> 120 us  [exchange(): pl.pallas_call(functools.partial(exchange_kernel, chunk, ahead), out_shap...]
where the time goes in v3:
time: 145 us; the launch traced here: 144 us
  Pallas kernels  135 us (93%)
  other arithmetic  5.15 us (4%)
  local copies, waits for them, and re-layouts  3.22 us (2%)
    pallas_call x1, Pallas kernels, exchange(): pl.pallas_call(functools.partial(exchange_kernel, chunk, ahead), out_shap...  120 us
    pallas_call x1, Pallas kernels, prepare(): pl.pallas_call(functools.partial(prepare_kernel, owners, owned), grid=(pa...  15.8 us
    convert_element_type x1, other arithmetic, on_device(): return spectra.reshape(owned, 2, 2, *spectra.shape[3:]).astype(F32)  4.5 us
    unnamed x6, local copies, waits for them, and re-layouts  3.22 us

profile of v3, /device:TPU:0, one launch (start us, length us, event | category | flops | bytes accessed | tf_op | source)
XLA Modules:
  0.0 143.8 jit_solution(10713868668922988609)
XLA Ops:
  0.0 0.7 convert_divide_fusion.inverse_ref
  0.7 0.0 copy-start.2
  0.7 0.7 copy-done.2
  1.3 15.8 %shard_map.37 = (bf16[8,4,256,768]{3,2,1,0:T(8,128)(2,1)}, bf16[8,4,2,16,768]{4,3,2,1,0:T(8,128)(2,1)S(1)}, bf16[8,6,2,16,768]{4,3,2,1,0:T(8,128)(2,1)S(1)}) custom-call(s32[8]{0:T(128)S(1)} %copy-done.2, f32[8]{0:T(128)S(1)} %convert_divide_fusion.inverse_ref, bf16[8,2,128,3072]{3,2,1,0:T(8,128)(2,1)} %x_ref.1), custom_call_target="tpu_custom_call" | custom-call | tf_op jit(solution)/shard_map/pallas_call | solution.py:108
  17.2 0.0 copy-start
  17.2 1.4 copy-done
  18.6 0.0 copy-start.1
  18.6 1.2 copy-done.1
  19.7 119.5 %shard_map.38 = bf16[12,4,4,16,384]{4,3,2,1,0:T(8,128)(2,1)} custom-call(bf16[8,4,2,16,768]{4,3,2,1,0:T(8,128)(2,1)} %copy-done.1, bf16[8,6,2,16,768]{4,3,2,1,0:T(8,128)(2,1)} %copy-done, bf16[8,4,256,768]{3,2,1,0:T(8,128)(2,1)} %get-tuple-element.10.y, bf16[12,4,2,128,384]{4,3,2,1,0:T(8,128)(2,1)} %bitcast.4), custom_call_target="tpu_custom_call" | custom-call | tf_op jit(solution)/shard_map/pallas_call | solution.py:444
  139.3 4.5 %convert.1 = f32[48,2,2,16,384]{4,3,2,1,0:T(8,128)} convert(bf16[48,2,2,16,384]{4,3,2,1,0:T(8,128)(2,1)} %bitcast.3) | non-fusion elementwise | flops 1179648 | bytes 7077888 | tf_op jit(solution)/shard_map/convert_element_type | solution.py:490
Async XLA Ops:
  0.7 0.7 copy-start.2
  17.2 1.4 copy-start
  18.6 1.2 copy-start.1

commit v4 on v3

v4 whole, which is shorter than its diff:
```python
import functools

import jax
import jax.numpy as jnp
from jax import lax
from jax.experimental import pallas as pl
from jax.experimental.pallas import tpu as pltpu
from jax.sharding import PartitionSpec as P

F32 = jnp.float32
BF16 = jnp.bfloat16
COS = (1.0, -19.73920440673828, 64.9390869140625, -85.4496078491211, 60.16310119628906, -25.950063705444336, 6.50340461730957)
SIN = (6.283182621002197, -41.341392517089844, 81.59541320800781, -76.57229614257812, 41.17121124267578, -12.217327117919922)
LANES = 128
ROWS = 4
MESH = pl.DeviceIdType.MESH


def poly(coefs, z):
    out = jnp.full_like(z, coefs[-1])
    for coef in coefs[-2::-1]:
        out = out * z + coef
    return out


def cos_sin(products, count, inverse):
    turns = jnp.floor(products * inverse + 0.5)
    t = (products - turns * count) * inverse
    z = t * t
    return poly(COS, z), t * poly(SIN, z)


def fill_table(table, halves, owners, coarse, fine):
    for step in range(halves):
        for j, (k, l) in enumerate(((0, 0), (1, 0), (0, 1), (1, 1))):
            table[pl.ds((4 * step + j) * owners, owners), :] = coarse(k) * fine(step, l)


def transform_waves(table, rows, parts, halves, owners):
    sums = lax.dot_general(table[...], rows, (((1,), (1,)), ((), ())), preferred_element_type=F32)
    width = rows.shape[0] // parts
    found = []
    for step in range(halves):
        for part in range(parts):
            at = slice(part * width, (part + 1) * width)
            cc, sc, cs, ss = (sums[(4 * step + j) * owners : (4 * step + j + 1) * owners, at] for j in range(4))
            found.append((cc - ss, sc + cs, cc + ss, sc - cs))
    return found


def keep_wave(total, spot, fields, t, real, imag):
    for r, value in enumerate((real, imag)):
        for s in range(2):
            total[4 * t + 2 * r + s, spot, :] = value[:, s * fields : (s + 1) * fields]


def pack_waves(total, groups, owners, pairs, fields, store):
    def pack(t, carry):
        for s in range(2):
            real = total[4 * t + s].reshape(owners, pairs, fields)
            imag = total[4 * t + 2 + s].reshape(owners, pairs, fields)
            store(t, s, jnp.concatenate([real, imag], axis=1).astype(BF16))
        return carry

    lax.fori_loop(0, groups, pack, 0)


def prepare_kernel(owners, owned, counts_ref, x_ref, y_ref, coarse_ref, fine_ref, folded_ref, sum_ref, table, total):
    pair = pl.program_id(0)
    count = counts_ref[pair]
    quarter = lax.shift_right_logical(count, 2)
    fields, points = x_ref.shape[1:]
    width = points // 4
    tiles = width // LANES
    last = points - width - LANES
    rows = 16
    lane = lax.broadcasted_iota(jnp.int32, (rows, LANES), 1)
    starts, shifts = [], []
    for k in range(4):
        start = jnp.minimum(quarter * k // LANES * LANES, last)
        starts.append(start)
        shifts.append(quarter * k - start)

    def fold(step, carry):
        row = pl.ds(pl.multiple_of(step * rows, rows), rows)
        keeps = [lane < LANES - shifts[k] for k in range(4)]

        def turned(k, h, i):
            v = x_ref[h, row, pl.ds(pl.multiple_of(starts[k] + i * LANES, LANES), LANES)]
            return pltpu.roll(v, (LANES - shifts[k]) & (LANES - 1), 1) if k else v

        before = {(k, h): turned(k, h, 0) for k in range(1, 4) for h in range(2)}
        for i in range(tiles):
            at = pl.ds(i * LANES, LANES)
            quarters = []
            for k in range(4):
                both = []
                for h in range(2):
                    if k:
                        after = turned(k, h, i + 1)
                        v = jnp.where(keeps[k], before[k, h], after)
                        before[k, h] = after
                    else:
                        v = turned(k, h, i)
                    both.append(v.astype(F32))
                quarters.append((both[0] + both[1], both[0] - both[1]))
            inside = lane + i * LANES < quarter
            for s in range(2):
                to = pl.ds(pl.multiple_of(step * rows + s * fields, rows), rows)
                x0, x1, x2, x3 = (quarters[k][s] for k in range(4))
                even, odd = x0 + x2, x1 + x3
                for kind, v in enumerate((even + odd, x0 - x2, even - odd, x1 - x3)):
                    if (i + 1) * LANES > points // 8:
                        v = jnp.where(inside, v, 0.0)
                    if kind:
                        y_ref[kind - 1, to, at] = v.astype(BF16)
                    else:
                        sum_ref[to, at] = v.astype(BF16)
        return carry

    lax.fori_loop(0, fields // rows, fold, 0, unroll=2)

    n = count.astype(F32)
    inverse = 1.0 / jnp.full((16, width), n, F32)
    groups = owned // 4
    middle = 2 * groups - 2
    place = lax.broadcasted_iota(jnp.int32, (16, width), 1).astype(F32)
    row = lax.broadcasted_iota(jnp.int32, (16, width), 0).astype(F32)
    rates = jnp.where(row < 8, 4 * row + 2, row + float(middle - 8))
    near_cos, near_sin = cos_sin(place * rates, n, inverse)
    fine_ref[0] = near_cos[:8]
    fine_ref[1] = near_sin[:8]
    owner_cos, owner_sin = cos_sin(place * (row * float(owned)), n, inverse)
    owner_cos, owner_sin = owner_cos * inverse, owner_sin * inverse
    for u in range(4):
        c, s = near_cos[8 + u : 9 + u], near_sin[8 + u : 9 + u]
        far = (owner_cos * c - owner_sin * s).astype(BF16), (owner_sin * c + owner_cos * s).astype(BF16)
        if u:
            coarse_ref[u - 1, 0], coarse_ref[u - 1, 1] = far
        else:
            halves = groups // 2
            near = near_cos, near_sin

            def fine(step, l):
                return jnp.broadcast_to(near[l][step : step + 1], (16, width)).astype(BF16)

            fill_table(table, halves, owners, lambda k: far[k], fine)
            spot = pl.ds(pair, owners, stride=8)
            waves = transform_waves(table, sum_ref[...], 1, halves, owners)
            for step, (ca, sa, da, ta) in enumerate(waves):
                keep_wave(total, spot, fields, halves + step, ca, -sa)
                keep_wave(total, spot, fields, halves - 1 - step, da, -ta)

    @pl.when(pair == pl.num_programs(0) - 1)
    def _():
        def store(t, s, value):
            folded_ref[:, t, s] = value

        pack_waves(total, groups, owners, 8, fields, store)


def prepare(grid_values, lon_counts, owners, owned):
    pairs, _, fields, points = grid_values.shape
    width = points // 4
    groups = owned // 4
    smem = pl.BlockSpec(memory_space=pltpu.SMEM)
    folded = (owners, groups, 2, 2 * pairs, fields)
    return pl.pallas_call(
        functools.partial(prepare_kernel, owners, owned),
        grid=(pairs,),
        out_shape=(
            jax.ShapeDtypeStruct((pairs, 3, 2 * fields, width), BF16),
            jax.ShapeDtypeStruct((pairs, 3, 2, owners, width), BF16),
            jax.ShapeDtypeStruct((pairs, 2, 8, width), F32),
            jax.ShapeDtypeStruct(folded, BF16),
        ),
        in_specs=[smem, pl.BlockSpec((None, 2, fields, points), lambda p: (p, 0, 0, 0))],
        out_specs=(
            pl.BlockSpec((None, 3, 2 * fields, width), lambda p: (p, 0, 0, 0)),
            pl.BlockSpec((None, 3, 2, owners, width), lambda p: (p, 0, 0, 0, 0)),
            pl.BlockSpec((None, 2, 8, width), lambda p: (p, 0, 0, 0)),
            pl.BlockSpec(folded, lambda p: (0, 0, 0, 0, 0)),
        ),
        scratch_shapes=[
            pltpu.VMEM((2 * fields, width), BF16),
            pltpu.VMEM((2 * groups * owners, width), BF16),
            pltpu.VMEM((4 * groups, owners * pairs, fields), F32),
        ],
        compiler_params=pltpu.CompilerParams(vmem_limit_bytes=60 * 2**20),
    )(lon_counts, grid_values)


def exchange_kernel(
    chunk, ahead, gap, far_hbm, near_hbm, first_class, y, legendre, out,
    near, far, samples, table, total, folded, inbox, weights, partial, from_core, first_out, from_first, second_out, from_second, staged,
    factor_sem, sample_sem, send_sem, recv_sem, weight_sem, core_send, core_recv, first_send, first_recv, second_send, second_recv, out_sem,
):
    _, owners, groups, _, both, fields = folded.shape
    degrees = legendre.shape[-1]
    pairs = both // 2
    per_class = groups // chunk
    chunks = 4 * per_class
    half = 2 * chunk
    block = fields // 8
    band, lev = lax.axis_index("band"), lax.axis_index("lev")
    chip, core = band // 2, band % 2
    beside = chip + 1 - 2 * (chip % 2)
    facing = 3 - chip
    opposite = (chip + 2) % 4
    first, second = (beside, facing), (facing, beside)
    sibling = {"band": chip * 2 + 1 - core}

    def on_chip(c):
        return {"band": c * 2 + core}

    def owner(d):
        return {"lev": d}

    def place(c):
        return c // per_class, pl.ds(c % per_class * chunk, chunk)

    count = y.shape[0]
    halves = groups // 2

    def sample(g, part):
        u, p = g // count, g % count
        kind = 2 if part else u % 2
        return pltpu.make_async_copy(y.at[p, kind], samples.at[g % 2, part], sample_sem.at[g % 2, part])

    def fetch(g):
        sample(g, 0).start()

        @pl.when(g // count % 2 == 0)
        def _():
            sample(g, 1).start()

    def transform(g):
        u, p = g // count, g % count

        @pl.when(g + 1 < 3 * count)
        def _():
            fetch(g + 1)

        def fine(step, l):
            return jnp.broadcast_to(near[p, l, step : step + 1, :], (owners, near.shape[-1])).astype(BF16)

        fill_table(table, halves, owners, lambda k: far[p, u, k], fine)
        keep = functools.partial(keep_wave, total, pl.ds(p, owners, stride=8), fields)
        sample(g, 0).wait()

        @pl.when(u == 1)
        def _():
            waves = transform_waves(table, samples[g % 2, 0], 1, halves, owners)
            for step, (ca, sa, da, ta) in enumerate(waves):
                keep(halves + step, ca, -sa)
                keep(halves - 1 - step, da, -ta)

        @pl.when(u != 1)
        def _():
            sample(g, 1).wait()
            sign = (1 - u).astype(F32)
            rows = samples[g % 2].reshape(4 * fields, samples.shape[-1])
            waves = iter(transform_waves(table, rows, 2, halves, owners))
            for step, ((ca, sa, da, ta), (cb, sb, db, tb)) in enumerate(zip(waves, waves)):
                keep(halves + step, ca - sign * sb, -(sa + sign * cb))
                keep(halves - 1 - step, da - sign * tb, -(ta + sign * db))

        @pl.when(p == count - 1)
        def _():
            def store(t, s, value):
                folded[u + 1, :, t, s] = value

            pack_waves(total, groups, owners, pairs, fields, store)

    def transform_part(q):
        u, i = q // per_class, q % per_class

        def one(p, carry):
            transform(u * count + p)
            return carry

        lax.fori_loop(i * count // per_class, (i + 1) * count // per_class, one, 0)

    fetch(0)
    factors = [
        pltpu.make_async_copy(source, target, factor_sem.at[i])
        for i, (source, target) in enumerate(((first_class, folded.at[0]), (far_hbm, far), (near_hbm, near)))
    ]
    for factor in factors:
        factor.start()
    barrier = pltpu.get_barrier_semaphore()
    for j in range(1, owners):
        pl.semaphore_signal(barrier, inc=1, device_id=owner((lev + j) % owners), device_id_type=MESH)
    for device in (sibling, on_chip(beside), on_chip(facing)):
        pl.semaphore_signal(barrier, inc=1, device_id=device, device_id_type=MESH)
    pl.semaphore_wait(barrier, owners + 2)

    def to_owner(c, d):
        u, t = place(c)
        return pltpu.make_async_remote_copy(
            src_ref=folded.at[u, d, t],
            dst_ref=inbox.at[c, lev],
            send_sem=send_sem.at[c, d],
            recv_sem=recv_sem.at[c, lev],
            device_id=owner(d),
            device_id_type=MESH,
        )

    def from_owner(c, d):
        u, t = place(c)
        return pltpu.make_async_remote_copy(
            src_ref=folded.at[u, d, t],
            dst_ref=inbox.at[c, d],
            send_sem=send_sem.at[c, d],
            recv_sem=recv_sem.at[c, d],
            device_id=owner(d),
            device_id_type=MESH,
        )

    def own(c):
        u, t = place(c)
        return pltpu.make_async_copy(folded.at[u, lev, t], inbox.at[c, lev], recv_sem.at[c, lev])

    def weight(c):
        u, t = place(c)
        return pltpu.make_async_copy(legendre.at[t, u], weights.at[c % (ahead + 1)], weight_sem.at[c])

    def across(c):
        return pltpu.make_async_remote_copy(
            src_ref=partial.at[c % (2 + 2 * gap), 1 - core],
            dst_ref=from_core.at[c],
            send_sem=core_send.at[c],
            recv_sem=core_recv.at[c],
            device_id=sibling,
            device_id_type=MESH,
        )

    def first_step(c, v):
        return pltpu.make_async_remote_copy(
            src_ref=first_out.at[c % (gap + 1), v],
            dst_ref=from_first.at[c, v],
            send_sem=first_send.at[c, v],
            recv_sem=first_recv.at[c, v],
            device_id=on_chip(first[v]),
            device_id_type=MESH,
        )

    def second_step(c, v):
        return pltpu.make_async_remote_copy(
            src_ref=second_out.at[c % (gap + 1), v],
            dst_ref=from_second.at[c, v],
            send_sem=second_send.at[c, v],
            recv_sem=second_recv.at[c, v],
            device_id=on_chip(second[v]),
            device_id_type=MESH,
        )

    def result(c):
        u, t = place(c)
        return pltpu.make_async_copy(staged.at[c % 2], out.at[t, u], out_sem.at[c])

    def launch(c):
        own(c).start()
        weight(c).start()

        def one(j, carry):
            to_owner(c, (lev + j) % owners).start()
            return carry

        lax.fori_loop(1, owners, one, 0)

    def sums(c):
        own(c).wait()
        weight(c).wait()

        def one(j, carry):
            from_owner(c, (lev + j) % owners).wait_recv()
            to_owner(c, (lev + j) % owners).wait_send()
            return carry

        lax.fori_loop(1, owners, one, 0)

        def wave(t, carry):
            for s in range(2):
                f = inbox[c, :, t, s].astype(F32).reshape(owners, 2, pairs, fields)
                part = jnp.concatenate(
                    [f[:, r].reshape(owners * pairs, fields) for r in range(2)], axis=1
                ).astype(BF16)
                total = lax.dot_general(
                    part, weights[c % (ahead + 1), t, s], (((0,), (0,)), ((), ())), preferred_element_type=F32
                ).astype(BF16)
                for r in range(2):
                    for b in range(8):
                        at = r * fields + b * block
                        partial[c % (2 + 2 * gap), b % 2, b // 2, 4 * t + 2 * s + r] = total[at : at + block]
            return carry

        lax.fori_loop(0, chunk, wave, 0)
        across(c).start()

    def parts(c, v, row, target):
        at = pl.ds(v * half + row, ROWS)
        return partial[c % (2 + 2 * gap), core, target, at].astype(F32) + from_core[c, target, at].astype(F32)

    def rows(body):
        def one(i, carry):
            body(i * ROWS)
            return carry

        lax.fori_loop(0, half // ROWS, one, 0)

    def first_stage(c):
        across(c).wait()
        for v in range(2):

            def add(row):
                for w, target in enumerate((first[v], opposite)):
                    first_out[c % (gap + 1), v, w, pl.ds(row, ROWS)] = parts(c, v, row, target).astype(BF16)

            rows(add)
            first_step(c, v).start()

    def second_stage(c):
        for v in range(2):
            first_step(c, v).wait()

            def add(row):
                at = pl.ds(row, ROWS)
                both = parts(c, v, row, second[v]) + from_first[c, v, 1, at].astype(F32)
                second_out[c % (gap + 1), v, at] = both.astype(BF16)

            rows(add)
            second_step(c, v).start()

    def last_stage(c):
        @pl.when(c >= 2)
        def _():
            result(c - 2).wait()

        for v in range(2):
            second_step(c, v).wait()

            def add(row):
                at = pl.ds(row, ROWS)
                both = parts(c, v, row, chip) + from_first[c, v, 0, at].astype(F32) + from_second[c, v, at].astype(F32)
                for i in range(ROWS // 4):
                    staged[c % 2, v * (chunk // 2) + row // 4 + i] = both[4 * i : 4 * i + 4]

            rows(add)
        result(c).start()

    factors[0].wait()
    for c in range(ahead):
        launch(c)
    factors[1].wait()
    factors[2].wait()
    for q in range(ahead - 1):
        transform_part(q)

    def turn(c, carry):
        @pl.when(c + ahead - 1 < 3 * per_class)
        def _():
            transform_part(c + ahead - 1)

        @pl.when(c + ahead < chunks)
        def _():
            launch(c + ahead)

        @pl.when(c < chunks)
        def _():
            sums(c)

        @pl.when((c >= 1) & (c <= chunks))
        def _():
            first_stage(c - 1)

        @pl.when((c >= 1 + gap) & (c <= chunks + gap))
        def _():
            second_stage(c - 1 - gap)

        @pl.when(c >= 1 + 2 * gap)
        def _():
            last_stage(c - 1 - 2 * gap)

        return carry

    lax.fori_loop(0, chunks + 1 + 2 * gap, turn, 0)
    result(chunks - 2).wait()
    result(chunks - 1).wait()


def exchange(y, coarse, fine, first_class, legendre, chunk, ahead, gap):
    count, _, columns, width = y.shape
    owners, fields, both = coarse.shape[3], columns // 2, 2 * count
    groups, _, _, latitudes, degrees = legendre.shape
    chunks = 4 * groups // chunk
    half = 2 * chunk
    block = fields // 8
    dma = pltpu.SemaphoreType.DMA
    anywhere = pl.BlockSpec(memory_space=pl.ANY)
    return pl.pallas_call(
        functools.partial(exchange_kernel, chunk, ahead, gap),
        out_shape=jax.ShapeDtypeStruct((groups, 4, 4, block, degrees), F32),
        in_specs=[anywhere] * 5,
        out_specs=anywhere,
        scratch_shapes=[
            pltpu.VMEM(fine.shape, F32),
            pltpu.VMEM(coarse.shape, BF16),
            pltpu.VMEM((2, 2, columns, width), BF16),
            pltpu.VMEM((2 * groups * owners, width), BF16),
            pltpu.VMEM((4 * groups, owners * count, fields), F32),
            pltpu.VMEM((4, owners, groups, 2, both, fields), BF16),
            pltpu.VMEM((chunks, owners, chunk, 2, both, fields), BF16),
            pltpu.VMEM((ahead + 1, chunk, 2, latitudes, degrees), BF16),
            pltpu.VMEM((2 + 2 * gap, 2, 4, 2 * half, block, degrees), BF16),
            pltpu.VMEM((chunks, 4, 2 * half, block, degrees), BF16),
            pltpu.VMEM((gap + 1, 2, 2, half, block, degrees), BF16),
            pltpu.VMEM((chunks, 2, 2, half, block, degrees), BF16),
            pltpu.VMEM((gap + 1, 2, half, block, degrees), BF16),
            pltpu.VMEM((chunks, 2, half, block, degrees), BF16),
            pltpu.VMEM((2, chunk, 4, block, degrees), F32),
            dma((3,)),
            dma((2, 2)),
            dma((chunks, owners)),
            dma((chunks, owners)),
            dma((chunks,)),
            dma((chunks,)),
            dma((chunks,)),
            dma((chunks, 2)),
            dma((chunks, 2)),
            dma((chunks, 2)),
            dma((chunks, 2)),
            dma((chunks,)),
        ],
        compiler_params=pltpu.CompilerParams(
            collective_id=0, has_side_effects=True, vmem_limit_bytes=60 * 2**20
        ),
    )(coarse, fine, first_class, y, legendre)


CHUNK = 2
AHEAD = 3
GAP = 2


def on_device(owners, grid_values, lon_counts, legendre):
    owned = legendre.shape[0]
    y, coarse, fine, first_class = prepare(grid_values, lon_counts, owners, owned)
    by_class = legendre.reshape(owned // 4, 4, *legendre.shape[1:])
    spectra = exchange(y, coarse, fine, first_class, by_class, CHUNK, AHEAD, GAP)
    return spectra.reshape(owned, 2, 2, *spectra.shape[3:])


def solution(mesh):
    return jax.shard_map(
        functools.partial(on_device, mesh.shape["lev"]),
        mesh=mesh,
        in_specs=(
            P(("band", "lev"), None, None, None),
            P(("band", "lev")),
            P("lev", None, "band", None),
        ),
        out_specs=P("lev", None, None, "band", None),
        check_vma=False,
    )
```

time: 145 us -> 130 us (0.90)
  Pallas kernels: 135 us -> 125 us
  other arithmetic: 5.15 us -> 0 us
  local copies, waits for them, and re-layouts: 3.22 us -> 5.17 us
    pallas_call x1, Pallas kernels: 120 us -> 108 us  [exchange(): pl.pallas_call(functools.partial(exchange_kernel, chunk, ahead, gap), out...]
    convert_element_type x1 -> x0, other arithmetic: 4.5 us -> none  [on_device(): return spectra.reshape(owned, 2, 2, *spectra.shape[3:]).astype(F32)]
    unnamed x6 -> x1, local copies, waits for them, and re-layouts: 3.22 us -> 5.17 us
where the time goes in v4:
time: 130 us
  Pallas kernels  125 us (96%)
  local copies, waits for them, and re-layouts  5.17 us (4%)
    pallas_call x1, Pallas kernels, exchange(): pl.pallas_call(functools.partial(exchange_kernel, chunk, ahead, gap), out...  108 us
    pallas_call x1, Pallas kernels, prepare(): pl.pallas_call(functools.partial(prepare_kernel, owners, owned), grid=(pa...  16.5 us
    unnamed x1, local copies, waits for them, and re-layouts  5.17 us

profile of v4, /device:TPU:0, one launch (start us, length us, event | category | flops | bytes accessed | tf_op | source)
XLA Modules:
  0.0 129.9 jit_solution(9590207042703015870)
XLA Ops:
  0.0 16.5 %shard_map.37 = (bf16[8,3,256,768]{3,2,1,0:T(8,128)(2,1)}, bf16[8,3,2,16,768]{4,3,2,1,0:T(8,128)(2,1)}, f32[8,2,8,768]{3,2,1,0:T(8,128)}, bf16[16,12,2,16,128]{4,3,2,1,0:T(8,128)(2,1)}) custom-call(s32[8]{0:T(128)} %counts_ref.1, bf16[8,2,128,3072]{3,2,1,0:T(8,128)(2,1)} %x_ref.1), custom_call_target="tpu_custom_call" | custom-call | tf_op jit(solution)/shard_map/pallas_call | solution.py:168
  16.5 108.2 %shard_map.38 = f32[12,4,4,16,384]{4,3,2,1,0:T(8,128)} custom-call(bf16[8,3,2,16,768]{4,3,2,1,0:T(8,128)(2,1)} %get-tuple-element.9.far_hbm, f32[8,2,8,768]{3,2,1,0:T(8,128)} %get-tuple-element.10.near_hbm, bf16[16,12,2,16,128]{4,3,2,1,0:T(8,128)(2,1)} %get-tuple-element.11.first_class, bf16[8,3,256,768]{3,2,1,0:T(8,128)(2,1)} %get-tuple-element.12.y, ...), custom_call_target="tpu_custom_call" | custom-call | tf_op jit(solution)/shard_map/pallas_call | solution.py:501
  124.7 5.2 %copy.5 = f32[48,2,2,16,384]{4,3,2,1,0:T(8,128)} copy(f32[48,2,2,16,384]{4,3,2,1,0:T(8,128)} %bitcast.2) | data formatting | bytes 9437184

commit v5 on v4

--- a/solution.py
+++ b/solution.py
@@ -186,13 +186,13 @@
             pltpu.VMEM((2 * groups * owners, width), BF16),
             pltpu.VMEM((4 * groups, owners * pairs, fields), F32),
         ],
-        compiler_params=pltpu.CompilerParams(vmem_limit_bytes=60 * 2**20),
+        compiler_params=pltpu.CompilerParams(vmem_limit_bytes=40 * 2**20),
     )(lon_counts, grid_values)
 
 
 def exchange_kernel(
     chunk, ahead, gap, far_hbm, near_hbm, first_class, y, legendre, out,
-    near, far, samples, table, total, folded, inbox, weights, partial, from_core, first_out, from_first, second_out, from_second, staged,
+    near, far, samples, table, total, folded, inbox, weights, crossing, partial, from_core, first_out, from_first, second_out, from_second, staged,
     factor_sem, sample_sem, send_sem, recv_sem, weight_sem, core_send, core_recv, first_send, first_recv, second_send, second_recv, out_sem,
 ):
     _, owners, groups, _, both, fields = folded.shape
@@ -225,7 +225,7 @@
     def sample(g, part):
         u, p = g // count, g % count
         kind = 2 if part else u % 2
-        return pltpu.make_async_copy(y.at[p, kind], samples.at[g % 2, part], sample_sem.at[g % 2, part])
+        return pltpu.make_async_copy(y.at[p, kind], samples.at[part], sample_sem.at[part])
 
     def fetch(g):
         sample(g, 0).start()
@@ -237,9 +237,7 @@
     def transform(g):
         u, p = g // count, g % count
 
-        @pl.when(g + 1 < 3 * count)
-        def _():
-            fetch(g + 1)
+        fetch(g)
 
         def fine(step, l):
             return jnp.broadcast_to(near[p, l, step : step + 1, :], (owners, near.shape[-1])).astype(BF16)
@@ -250,7 +248,7 @@
 
         @pl.when(u == 1)
         def _():
-            waves = transform_waves(table, samples[g % 2, 0], 1, halves, owners)
+            waves = transform_waves(table, samples[0], 1, halves, owners)
             for step, (ca, sa, da, ta) in enumerate(waves):
                 keep(halves + step, ca, -sa)
                 keep(halves - 1 - step, da, -ta)
@@ -259,7 +257,7 @@
         def _():
             sample(g, 1).wait()
             sign = (1 - u).astype(F32)
-            rows = samples[g % 2].reshape(4 * fields, samples.shape[-1])
+            rows = samples[...].reshape(4 * fields, samples.shape[-1])
             waves = iter(transform_waves(table, rows, 2, halves, owners))
             for step, ((ca, sa, da, ta), (cb, sb, db, tb)) in enumerate(zip(waves, waves)):
                 keep(halves + step, ca - sign * sb, -(sa + sign * cb))
@@ -268,7 +266,7 @@
         @pl.when(p == count - 1)
         def _():
             def store(t, s, value):
-                folded[u + 1, :, t, s] = value
+                folded[(u + 1) % 2, :, t, s] = value
 
             pack_waves(total, groups, owners, pairs, fields, store)
 
@@ -281,7 +279,6 @@
 
         lax.fori_loop(i * count // per_class, (i + 1) * count // per_class, one, 0)
 
-    fetch(0)
     factors = [
         pltpu.make_async_copy(source, target, factor_sem.at[i])
         for i, (source, target) in enumerate(((first_class, folded.at[0]), (far_hbm, far), (near_hbm, near)))
@@ -298,7 +295,7 @@
     def to_owner(c, d):
         u, t = place(c)
         return pltpu.make_async_remote_copy(
-            src_ref=folded.at[u, d, t],
+            src_ref=folded.at[u % 2, d, t],
             dst_ref=inbox.at[c, lev],
             send_sem=send_sem.at[c, d],
             recv_sem=recv_sem.at[c, lev],
@@ -309,7 +306,7 @@
     def from_owner(c, d):
         u, t = place(c)
         return pltpu.make_async_remote_copy(
-            src_ref=folded.at[u, d, t],
+            src_ref=folded.at[u % 2, d, t],
             dst_ref=inbox.at[c, d],
             send_sem=send_sem.at[c, d],
             recv_sem=recv_sem.at[c, d],
@@ -319,15 +316,15 @@
 
     def own(c):
         u, t = place(c)
-        return pltpu.make_async_copy(folded.at[u, lev, t], inbox.at[c, lev], recv_sem.at[c, lev])
+        return pltpu.make_async_copy(folded.at[u % 2, lev, t], inbox.at[c, lev], recv_sem.at[c, lev])
 
     def weight(c):
         u, t = place(c)
-        return pltpu.make_async_copy(legendre.at[t, u], weights.at[c % (ahead + 1)], weight_sem.at[c])
+        return pltpu.make_async_copy(legendre.at[t, u], weights.at[c % 2], weight_sem.at[c])
 
     def across(c):
         return pltpu.make_async_remote_copy(
-            src_ref=partial.at[c % (2 + 2 * gap), 1 - core],
+            src_ref=crossing.at[c % 2],
             dst_ref=from_core.at[c],
             send_sem=core_send.at[c],
             recv_sem=core_recv.at[c],
@@ -361,7 +358,6 @@
 
     def launch(c):
         own(c).start()
-        weight(c).start()
 
         def one(j, carry):
             to_owner(c, (lev + j) % owners).start()
@@ -387,12 +383,14 @@
                     [f[:, r].reshape(owners * pairs, fields) for r in range(2)], axis=1
                 ).astype(BF16)
                 total = lax.dot_general(
-                    part, weights[c % (ahead + 1), t, s], (((0,), (0,)), ((), ())), preferred_element_type=F32
+                    part, weights[c % 2, t, s], (((0,), (0,)), ((), ())), preferred_element_type=F32
                 ).astype(BF16)
                 for r in range(2):
-                    for b in range(8):
-                        at = r * fields + b * block
-                        partial[c % (2 + 2 * gap), b % 2, b // 2, 4 * t + 2 * s + r] = total[at : at + block]
+                    for b in range(4):
+                        at = r * fields + 2 * b * block
+                        even, odd = total[at : at + block], total[at + block : at + 2 * block]
+                        partial[c % (2 + 2 * gap), b, 4 * t + 2 * s + r] = jnp.where(core == 0, even, odd)
+                        crossing[c % 2, b, 4 * t + 2 * s + r] = jnp.where(core == 0, odd, even)
             return carry
 
         lax.fori_loop(0, chunk, wave, 0)
@@ -400,7 +398,7 @@
 
     def parts(c, v, row, target):
         at = pl.ds(v * half + row, ROWS)
-        return partial[c % (2 + 2 * gap), core, target, at].astype(F32) + from_core[c, target, at].astype(F32)
+        return partial[c % (2 + 2 * gap), target, at].astype(F32) + from_core[c, target, at].astype(F32)
 
     def rows(body):
         def one(i, carry):
@@ -457,7 +455,13 @@
     for q in range(ahead - 1):
         transform_part(q)
 
+    weight(0).start()
+
     def turn(c, carry):
+        @pl.when(c + 1 < chunks)
+        def _():
+            weight(c + 1).start()
+
         @pl.when(c + ahead - 1 < 3 * per_class)
         def _():
             transform_part(c + ahead - 1)
@@ -506,13 +510,14 @@
         scratch_shapes=[
             pltpu.VMEM(fine.shape, F32),
             pltpu.VMEM(coarse.shape, BF16),
-            pltpu.VMEM((2, 2, columns, width), BF16),
+            pltpu.VMEM((2, columns, width), BF16),
             pltpu.VMEM((2 * groups * owners, width), BF16),
             pltpu.VMEM((4 * groups, owners * count, fields), F32),
-            pltpu.VMEM((4, owners, groups, 2, both, fields), BF16),
+            pltpu.VMEM((2, owners, groups, 2, both, fields), BF16),
             pltpu.VMEM((chunks, owners, chunk, 2, both, fields), BF16),
-            pltpu.VMEM((ahead + 1, chunk, 2, latitudes, degrees), BF16),
-            pltpu.VMEM((2 + 2 * gap, 2, 4, 2 * half, block, degrees), BF16),
+            pltpu.VMEM((2, chunk, 2, latitudes, degrees), BF16),
+            pltpu.VMEM((2, 4, 2 * half, block, degrees), BF16),
+            pltpu.VMEM((2 + 2 * gap, 4, 2 * half, block, degrees), BF16),
             pltpu.VMEM((chunks, 4, 2 * half, block, degrees), BF16),
             pltpu.VMEM((gap + 1, 2, 2, half, block, degrees), BF16),
             pltpu.VMEM((chunks, 2, 2, half, block, degrees), BF16),
@@ -520,7 +525,7 @@
             pltpu.VMEM((chunks, 2, half, block, degrees), BF16),
             pltpu.VMEM((2, chunk, 4, block, degrees), F32),
             dma((3,)),
-            dma((2, 2)),
+            dma((2,)),
             dma((chunks, owners)),
             dma((chunks, owners)),
             dma((chunks,)),
@@ -533,7 +538,7 @@
             dma((chunks,)),
         ],
         compiler_params=pltpu.CompilerParams(
-            collective_id=0, has_side_effects=True, vmem_limit_bytes=60 * 2**20
+            collective_id=0, has_side_effects=True, vmem_limit_bytes=37 * 2**20
         ),
     )(coarse, fine, first_class, y, legendre)
 

time: 130 us -> 125 us (0.962)
  Pallas kernels: 125 us -> 122 us
  local copies, waits for them, and re-layouts: 5.17 us -> 2.84 us
    pallas_call x1, Pallas kernels: 16.5 us -> 13.2 us  [prepare(): pl.pallas_call(functools.partial(prepare_kernel, owners, owned), grid=(pa...]
    unnamed x1 -> x3, local copies, waits for them, and re-layouts: 5.17 us -> 2.84 us
where the time goes in v5:
time: 125 us; the launch traced here: 124 us
  Pallas kernels  122 us (98%)
  local copies, waits for them, and re-layouts  2.84 us (2%)
    pallas_call x1, Pallas kernels, exchange(): pl.pallas_call(functools.partial(exchange_kernel, chunk, ahead, gap), out...  108 us
    pallas_call x1, Pallas kernels, prepare(): pl.pallas_call(functools.partial(prepare_kernel, owners, owned), grid=(pa...  13.2 us
    unnamed x3, local copies, waits for them, and re-layouts  2.84 us

profile of v5, /device:TPU:0, one launch (start us, length us, event | category | flops | bytes accessed | tf_op | source)
XLA Modules:
  0.0 124.5 jit_solution(16207250505113275375)
XLA Ops:
  0.0 0.0 copy-start
  0.0 0.7 copy-done
  0.7 13.2 %shard_map.37 = (bf16[8,3,256,768]{3,2,1,0:T(8,128)(2,1)S(1)}, bf16[8,3,2,16,768]{4,3,2,1,0:T(8,128)(2,1)S(1)}, f32[8,2,8,768]{3,2,1,0:T(8,128)S(1)}, bf16[16,12,2,16,128]{4,3,2,1,0:T(8,128)(2,1)S(1)}) custom-call(s32[8]{0:T(128)S(1)} %copy-done, bf16[8,2,128,3072]{3,2,1,0:T(8,128)(2,1)} %x_ref.1), custom_call_target="tpu_custom_call" | custom-call | tf_op jit(solution)/shard_map/pallas_call | solution.py:168
  13.9 108.4 %shard_map.38 = f32[12,4,4,16,384]{4,3,2,1,0:T(8,128)S(1)} custom-call(bf16[8,3,2,16,768]{4,3,2,1,0:T(8,128)(2,1)S(1)} %get-tuple-element.9.far_hbm, f32[8,2,8,768]{3,2,1,0:T(8,128)S(1)} %get-tuple-element.10.near_hbm, bf16[16,12,2,16,128]{4,3,2,1,0:T(8,128)(2,1)S(1)} %get-tuple-element.11.first_class, bf16[8,3,256,768]{3,2,1,0:T(8,128)(2,1)S(1)} %get-tuple-element.12.y, ...), custom_call_target="tpu_custom_call" | custom-call | tf_op jit(solution)/shard_map/pallas_call | solution.py:505
  122.3 2.2 %copy.5 = f32[48,2,2,16,384]{4,3,2,1,0:T(8,128)} copy(f32[48,2,2,16,384]{4,3,2,1,0:T(8,128)S(1)} %bitcast.2) | data formatting | bytes 9437184
Async XLA Ops:
  0.0 0.7 copy-start

commit v6 on v5

--- a/solution.py
+++ b/solution.py
@@ -13,6 +13,7 @@
 SIN = (6.283182621002197, -41.341392517089844, 81.59541320800781, -76.57229614257812, 41.17121124267578, -12.217327117919922)
 LANES = 128
 ROWS = 4
+TOGETHER = 2
 MESH = pl.DeviceIdType.MESH
 
 
@@ -65,8 +66,24 @@
     lax.fori_loop(0, groups, pack, 0)
 
 
-def prepare_kernel(owners, owned, counts_ref, x_ref, y_ref, coarse_ref, fine_ref, folded_ref, sum_ref, table, total):
-    pair = pl.program_id(0)
+def prepare_kernel(owned, counts_ref, x_ref, y_ref, coarse_ref, fine_ref, folded_ref, sum_ref, table, total):
+    together = x_ref.shape[0]
+    for i in range(together):
+        refs = (ref.at[i] for ref in (x_ref, y_ref, coarse_ref, fine_ref, sum_ref, table))
+        prepare_pair(pl.program_id(0) * together + i, owned, counts_ref, *refs, total)
+
+    @pl.when(pl.program_id(0) == pl.num_programs(0) - 1)
+    def _():
+        owners, groups, _, both, fields = folded_ref.shape
+
+        def store(t, s, value):
+            folded_ref[:, t, s] = value
+
+        pack_waves(total, groups, owners, both // 2, fields, store)
+
+
+def prepare_pair(pair, owned, counts_ref, x_ref, y_ref, coarse_ref, fine_ref, sum_ref, table, total):
+    owners = coarse_ref.shape[2]
     count = counts_ref[pair]
     quarter = lax.shift_right_logical(count, 2)
     fields, points = x_ref.shape[1:]
@@ -102,7 +119,7 @@
                         before[k, h] = after
                     else:
                         v = turned(k, h, i)
-                    both.append(v.astype(F32))
+                    both.append(v)
                 quarters.append((both[0] + both[1], both[0] - both[1]))
             inside = lane + i * LANES < quarter
             for s in range(2):
@@ -111,14 +128,14 @@
                 even, odd = x0 + x2, x1 + x3
                 for kind, v in enumerate((even + odd, x0 - x2, even - odd, x1 - x3)):
                     if (i + 1) * LANES > points // 8:
-                        v = jnp.where(inside, v, 0.0)
+                        v = jnp.where(inside, v, jnp.zeros_like(v))
                     if kind:
                         y_ref[kind - 1, to, at] = v.astype(BF16)
                     else:
                         sum_ref[to, at] = v.astype(BF16)
         return carry
 
-    lax.fori_loop(0, fields // rows, fold, 0, unroll=2)
+    lax.fori_loop(0, fields // rows, fold, 0, unroll=8)
 
     n = count.astype(F32)
     inverse = 1.0 / jnp.full((16, width), n, F32)
@@ -151,13 +168,6 @@
                 keep_wave(total, spot, fields, halves + step, ca, -sa)
                 keep_wave(total, spot, fields, halves - 1 - step, da, -ta)
 
-    @pl.when(pair == pl.num_programs(0) - 1)
-    def _():
-        def store(t, s, value):
-            folded_ref[:, t, s] = value
-
-        pack_waves(total, groups, owners, 8, fields, store)
-
 
 def prepare(grid_values, lon_counts, owners, owned):
     pairs, _, fields, points = grid_values.shape
@@ -166,24 +176,24 @@
     smem = pl.BlockSpec(memory_space=pltpu.SMEM)
     folded = (owners, groups, 2, 2 * pairs, fields)
     return pl.pallas_call(
-        functools.partial(prepare_kernel, owners, owned),
-        grid=(pairs,),
+        functools.partial(prepare_kernel, owned),
+        grid=(pairs // TOGETHER,),
         out_shape=(
             jax.ShapeDtypeStruct((pairs, 3, 2 * fields, width), BF16),
             jax.ShapeDtypeStruct((pairs, 3, 2, owners, width), BF16),
             jax.ShapeDtypeStruct((pairs, 2, 8, width), F32),
             jax.ShapeDtypeStruct(folded, BF16),
         ),
-        in_specs=[smem, pl.BlockSpec((None, 2, fields, points), lambda p: (p, 0, 0, 0))],
+        in_specs=[smem, pl.BlockSpec((TOGETHER, 2, fields, points), lambda p: (p, 0, 0, 0))],
         out_specs=(
-            pl.BlockSpec((None, 3, 2 * fields, width), lambda p: (p, 0, 0, 0)),
-            pl.BlockSpec((None, 3, 2, owners, width), lambda p: (p, 0, 0, 0, 0)),
-            pl.BlockSpec((None, 2, 8, width), lambda p: (p, 0, 0, 0)),
+            pl.BlockSpec((TOGETHER, 3, 2 * fields, width), lambda p: (p, 0, 0, 0)),
+            pl.BlockSpec((TOGETHER, 3, 2, owners, width), lambda p: (p, 0, 0, 0, 0)),
+            pl.BlockSpec((TOGETHER, 2, 8, width), lambda p: (p, 0, 0, 0)),
             pl.BlockSpec(folded, lambda p: (0, 0, 0, 0, 0)),
         ),
         scratch_shapes=[
-            pltpu.VMEM((2 * fields, width), BF16),
-            pltpu.VMEM((2 * groups * owners, width), BF16),
+            pltpu.VMEM((TOGETHER, 2 * fields, width), BF16),
+            pltpu.VMEM((TOGETHER, 2 * groups * owners, width), BF16),
             pltpu.VMEM((4 * groups, owners * pairs, fields), F32),
         ],
         compiler_params=pltpu.CompilerParams(vmem_limit_bytes=40 * 2**20),
@@ -292,10 +302,10 @@
         pl.semaphore_signal(barrier, inc=1, device_id=device, device_id_type=MESH)
     pl.semaphore_wait(barrier, owners + 2)
 
-    def to_owner(c, d):
+    def to_owner(c, d, early=False):
         u, t = place(c)
         return pltpu.make_async_remote_copy(
-            src_ref=folded.at[u % 2, d, t],
+            src_ref=first_class.at[d, t] if early else folded.at[u % 2, d, t],
             dst_ref=inbox.at[c, lev],
             send_sem=send_sem.at[c, d],
             recv_sem=recv_sem.at[c, lev],
@@ -314,9 +324,10 @@
             device_id_type=MESH,
         )
 
-    def own(c):
+    def own(c, early=False):
         u, t = place(c)
-        return pltpu.make_async_copy(folded.at[u % 2, lev, t], inbox.at[c, lev], recv_sem.at[c, lev])
+        source = first_class.at[lev, t] if early else folded.at[u % 2, lev, t]
+        return pltpu.make_async_copy(source, inbox.at[c, lev], recv_sem.at[c, lev])
 
     def weight(c):
         u, t = place(c)
@@ -356,11 +367,11 @@
         u, t = place(c)
         return pltpu.make_async_copy(staged.at[c % 2], out.at[t, u], out_sem.at[c])
 
-    def launch(c):
-        own(c).start()
+    def launch(c, early=False):
+        own(c, early).start()
 
         def one(j, carry):
-            to_owner(c, (lev + j) % owners).start()
+            to_owner(c, (lev + j) % owners, early).start()
             return carry
 
         lax.fori_loop(1, owners, one, 0)
@@ -447,16 +458,14 @@
             rows(add)
         result(c).start()
 
-    factors[0].wait()
+    weight(0).start()
     for c in range(ahead):
-        launch(c)
-    factors[1].wait()
-    factors[2].wait()
+        launch(c, True)
+    for factor in factors:
+        factor.wait()
     for q in range(ahead - 1):
         transform_part(q)
 
-    weight(0).start()
-
     def turn(c, carry):
         @pl.when(c + 1 < chunks)
         def _():
@@ -470,21 +479,21 @@
         def _():
             launch(c + ahead)
 
+        @pl.when((c >= 1) & (c <= chunks))
+        def _():
+            first_stage(c - 1)
+
+        @pl.when((c >= 1 + gap) & (c <= chunks + gap))
+        def _():
+            second_stage(c - 1 - gap)
+
+        @pl.when(c >= 1 + 2 * gap)
+        def _():
+            last_stage(c - 1 - 2 * gap)
+
         @pl.when(c < chunks)
         def _():
             sums(c)
-
-        @pl.when((c >= 1) & (c <= chunks))
-        def _():
-            first_stage(c - 1)
-
-        @pl.when((c >= 1 + gap) & (c <= chunks + gap))
-        def _():
-            second_stage(c - 1 - gap)
-
-        @pl.when(c >= 1 + 2 * gap)
-        def _():
-            last_stage(c - 1 - 2 * gap)
 
         return carry
 

time: 125 us -> 121 us (0.968)
  Pallas kernels: 122 us -> 118 us
    pallas_call x1, Pallas kernels: 13.2 us -> 10 us  [prepare(): pl.pallas_call(functools.partial(prepare_kernel, owned), grid=(pairs // T...]
where the time goes in v6:
time: 121 us
  Pallas kernels  118 us (98%)
  local copies, waits for them, and re-layouts  2.84 us (2%)
    pallas_call x1, Pallas kernels, exchange(): pl.pallas_call(functools.partial(exchange_kernel, chunk, ahead, gap), out...  108 us
    pallas_call x1, Pallas kernels, prepare(): pl.pallas_call(functools.partial(prepare_kernel, owned), grid=(pairs // T...  10 us
    unnamed x3, local copies, waits for them, and re-layouts  2.84 us

profile of v6, /device:TPU:0, one launch (start us, length us, event | category | flops | bytes accessed | tf_op | source)
XLA Modules:
  0.0 120.7 jit_solution(11112503045089856687)
XLA Ops:
  0.0 0.0 copy-start
  0.0 0.7 copy-done
  0.7 10.0 %shard_map.37 = (bf16[8,3,256,768]{3,2,1,0:T(8,128)(2,1)S(1)}, bf16[8,3,2,16,768]{4,3,2,1,0:T(8,128)(2,1)S(1)}, f32[8,2,8,768]{3,2,1,0:T(8,128)S(1)}, bf16[16,12,2,16,128]{4,3,2,1,0:T(8,128)(2,1)S(1)}) custom-call(s32[8]{0:T(128)S(1)} %copy-done, bf16[8,2,128,3072]{3,2,1,0:T(8,128)(2,1)} %x_ref.1), custom_call_target="tpu_custom_call" | custom-call | tf_op jit(solution)/shard_map/pallas_call | solution.py:178
  10.7 107.9 %shard_map.38 = f32[12,4,4,16,384]{4,3,2,1,0:T(8,128)S(1)} custom-call(bf16[8,3,2,16,768]{4,3,2,1,0:T(8,128)(2,1)S(1)} %get-tuple-element.9.far_hbm, f32[8,2,8,768]{3,2,1,0:T(8,128)S(1)} %get-tuple-element.10.near_hbm, bf16[16,12,2,16,128]{4,3,2,1,0:T(8,128)(2,1)S(1)} %get-tuple-element.11.first_class, bf16[8,3,256,768]{3,2,1,0:T(8,128)(2,1)S(1)} %get-tuple-element.12.y, ...), custom_call_target="tpu_custom_call" | custom-call | tf_op jit(solution)/shard_map/pallas_call | solution.py:514
  118.6 2.2 %copy.5 = f32[48,2,2,16,384]{4,3,2,1,0:T(8,128)} copy(f32[48,2,2,16,384]{4,3,2,1,0:T(8,128)S(1)} %bitcast.2) | data formatting | bytes 9437184
Async XLA Ops:
  0.0 0.7 copy-start
